TPU v7x, 32 devices: a whole 2x2x4 slice. The times are simulated.
32 devices in a mesh: dp: 4 (over y, x), expert: 8 (over z, core).
Axes of the slice: x: 2, y: 2, z: 4, core: 2. Of those that a mesh axis runs over, the one named last changes fastest.
Arguments:
- tokens: bfloat16 [4096, 2048], P(('dp', 'expert')), may hold values from -6 to 6
- cotangent: bfloat16 [4096, 2048], P(('dp', 'expert')), may hold values from -6 to 6
- gate_probs: float32 [4096, 2], P(('dp', 'expert')), may hold values from 0.05 to 1
- expert_ids: int32 [4096, 2], P(('dp', 'expert')), may hold values from 0 to 7, all different within a row; in each aligned block of 128 rows (0 to 127, 128 to 255, ...) at most 40 rows name the same one
- gate_up: bfloat16 [8, 2048, 1536], P('expert'), may hold values from -0.125 to 0.125
- down: bfloat16 [8, 768, 2048], P('expert'), may hold values from -0.21875 to 0.21875
Outputs:
- grad_probs: float32 [4096, 2], P(('dp', 'expert'))
- grad_gate_up: bfloat16 [8, 2048, 1536], P('expert', 'dp')
- grad_down: bfloat16 [8, 768, 2048], P('expert', None, 'dp')
Inputs may be any that keep to these rules, and one draw needn't show every extreme that they name: `expert_ids`: each token names 2 different experts. Among the 128 rows of one device no expert is named more than 40 times, and in every draw some expert is named exactly 40 times by the rows of some device.
All inputs are finite; a program needn't handle non-finite values.
Results may differ from a plain program's by a relative error of at most 0.025.
Values may be sent and summed in bfloat16 or wider, within the bound.
No kernel may reach another device: no remote copies, remote signals or barrier semaphores. Data moves between devices by JAX's collectives and lax.ppermute only.
A program may use at most 128 MiB of HBM per device.

v0:
```python
import jax
import jax.numpy as jnp
from jax import lax
from jax.sharding import PartitionSpec as P

EXPERTS = 8
CAP = 40


def widen(values, slices, expert_count):
    tail = values.shape[1:]
    spread = values.reshape((EXPERTS, 1, CAP) + tail)
    spread = jnp.broadcast_to(spread, (EXPERTS, slices, CAP) + tail)
    return spread.reshape((expert_count, CAP) + tail)


def forward_part(rows_x, weight_gu, half):
    both_pre = jnp.dot(rows_x, weight_gu, preferred_element_type=jnp.float32)
    gate_pre = both_pre[:, :half]
    up_pre = both_pre[:, half:]
    activated = jax.nn.silu(gate_pre)
    hidden = (activated * up_pre).astype(jnp.bfloat16)
    return (gate_pre, up_pre, activated, hidden)


def backward_part(rows_x, rows_dy, rows_p, weight_gu, weight_down, half):
    gate_pre, up_pre, activated, hidden = forward_part(rows_x, weight_gu, half)
    expert_out = jnp.dot(hidden, weight_down, preferred_element_type=jnp.float32)
    dy_wide = rows_dy.astype(jnp.float32)
    inner = jnp.sum(expert_out * dy_wide, axis=1)
    scaled = (rows_p[:, None] * dy_wide).astype(jnp.bfloat16)
    grad_down = lax.dot_general(
        hidden, scaled, (((0,), (0,)), ((), ())), preferred_element_type=jnp.float32
    )
    grad_hidden = lax.dot_general(
        scaled, weight_down, (((1,), (1,)), ((), ())), preferred_element_type=jnp.float32
    )
    sigmoid_gate = jax.nn.sigmoid(gate_pre)
    grad_gate_pre = (
        grad_hidden * up_pre * sigmoid_gate * (1.0 + gate_pre * (1.0 - sigmoid_gate))
    ).astype(jnp.bfloat16)
    grad_up_pre = (grad_hidden * activated).astype(jnp.bfloat16)
    grad_both = jnp.concatenate([grad_gate_pre, grad_up_pre], axis=1)
    grad_gu = lax.dot_general(
        rows_x, grad_both, (((0,), (0,)), ((), ())), preferred_element_type=jnp.float32
    )
    return (grad_gu, grad_down, inner)


def body(tokens, cotangent, gate_probs, expert_ids, gate_up, down):
    expert_count = lax.axis_size("expert")
    slices = expert_count // EXPERTS
    tok_count = tokens.shape[0]
    choose_count = expert_ids.shape[1]
    half = gate_up.shape[2] // 2
    width = tokens.shape[1]
    slot_rows = EXPERTS * CAP
    flat_ids = expert_ids.reshape(-1)
    expert_range = jnp.arange(EXPERTS, dtype=jnp.int32)
    choose = (flat_ids[:, None] == expert_range[None, :]).astype(jnp.int32)
    earlier = jnp.cumsum(choose, axis=0) - choose
    position = jnp.sum(earlier * choose, axis=1)
    slot_of = flat_ids * CAP + position
    picked = jnp.arange(slot_rows, dtype=jnp.int32)[:, None] == slot_of[None, :]
    picked_tok = jnp.any(picked.reshape(slot_rows, tok_count, choose_count), axis=2).astype(
        jnp.bfloat16
    )
    local_x = jnp.dot(picked_tok, tokens, preferred_element_type=jnp.float32).astype(jnp.bfloat16)
    local_dy = jnp.dot(picked_tok, cotangent, preferred_element_type=jnp.float32).astype(
        jnp.bfloat16
    )
    flat_probs = gate_probs.reshape(-1)
    own_prob = jnp.where(flat_ids == flat_ids, flat_probs, 0.0)
    lent_prob = jnp.where(flat_ids == flat_ids, 0.0, flat_probs)
    slot_own = jnp.sum(jnp.where(picked, own_prob[None, :], 0.0), axis=1)
    slot_lent = jnp.sum(jnp.where(picked, lent_prob[None, :], 0.0), axis=1)
    send_x = widen(local_x, slices, expert_count)
    send_dy = widen(local_dy, slices, expert_count)
    send_own = widen(slot_own, slices, expert_count)
    send_lent = widen(slot_lent, slices, expert_count)
    weight_gu = gate_up[0]
    weight_down = down[0]
    recv_x, recv_dy, recv_own, recv_lent = (
        lax.all_to_all(send_x, "expert", split_axis=0, concat_axis=0, tiled=True),
        lax.all_to_all(send_dy, "expert", split_axis=0, concat_axis=0, tiled=True),
        lax.all_to_all(
            send_own.astype(jnp.bfloat16), "expert", split_axis=0, concat_axis=0, tiled=True
        ).astype(send_own.dtype),
        lax.all_to_all(
            send_lent.astype(jnp.bfloat16), "expert", split_axis=0, concat_axis=0, tiled=True
        ).astype(send_lent.dtype),
    )
    rows_x = recv_x.reshape(expert_count * CAP, width)
    rows_dy = recv_dy.reshape(expert_count * CAP, width)
    rows_own = recv_own.reshape(expert_count * CAP)
    grad_gu, grad_down, inner_rows = backward_part(
        rows_x, rows_dy, rows_own, weight_gu, weight_down, half
    )
    returned = lax.all_to_all(
        inner_rows.reshape(expert_count, CAP), "expert", split_axis=0, concat_axis=0, tiled=True
    )
    per_slot = jnp.sum(returned.reshape(EXPERTS, slices, CAP), axis=1).reshape(slot_rows)
    grad_probs = jnp.sum(jnp.where(picked, per_slot[:, None], 0.0), axis=0).reshape(
        tok_count, choose_count
    )
    reduced_gu = lax.psum_scatter(
        grad_gu.astype(jnp.bfloat16), "dp", scatter_dimension=0, tiled=True
    )
    reduced_down = lax.psum_scatter(
        grad_down.astype(jnp.bfloat16), "dp", scatter_dimension=1, tiled=True
    )
    return (grad_probs, reduced_gu[None], reduced_down[None])


def solution(mesh):
    return jax.shard_map(
        body,
        mesh=mesh,
        in_specs=(
            P(("dp", "expert"), None),
            P(("dp", "expert"), None),
            P(("dp", "expert"), None),
            P(("dp", "expert"), None),
            P("expert", None, None),
            P("expert", None, None),
        ),
        out_specs=(P(("dp", "expert"), None), P("expert", "dp", None), P("expert", None, "dp")),
        check_vma=False,
    )
```

profile of v0, /device:TPU:0, one launch (start us, length us, event | category | flops | bytes accessed | tf_op | source)
XLA Modules:
  0.0 237.8 jit_solution(2803277563012913981)
XLA Ops:
  7.2 0.0 copy-start
  7.2 0.9 copy.37
  8.1 0.1 reshape.95
  8.3 0.1 eq.48
  8.4 0.6 reduce-window.6
  9.0 0.2 slice_reduce_fusion
  9.3 0.1 fusion.19
  9.3 0.1 reduce_sum.43
  9.5 0.1 copy.39
  9.6 0.7 multiply_add_fusion
  10.3 2.6 %convolution_convert_fusion.3 = bf16[320,2048]{1,0:T(8,128)(2,1)} fusion(pred[320,128]{1,0:T(8,128)(4,1)S(1)} %fusion.17, bf16[128,2048]{1,0:T(8,128)(2,1)} %param.6), kind=kOutput, calls=%fused_computation.10 | convolution fusion | flops 168427520 | bytes 1875968 | tf_op jit(solution)/shard_map/dot_general | solution.py:68
  12.9 6.3 %all-to-all-start = ((bf16[8,40,2048]{2,1,0:T(8,128)(2,1)}), bf16[8,40,2048]{2,1,0:T(8,128)(2,1)}, u32[]{:S(2)}, u32[]{:S(2)}) async-start(bf16[8,40,2048]{2,1,0:T(8,128)(2,1)} %bitcast.41), calls=%async_computation | async-start | bytes 2621440 | tf_op jit(solution)/shard_map/all_to_all | solution.py:84
  19.2 2.6 %convolution_convert_fusion.2 = bf16[320,2048]{1,0:T(8,128)(2,1)} fusion(pred[320,128]{1,0:T(8,128)(4,1)S(1)} %fusion.17, bf16[128,2048]{1,0:T(8,128)(2,1)} %param.7), kind=kOutput, calls=%fused_computation.9 | convolution fusion | flops 168427520 | bytes 1875968 | tf_op jit(solution)/shard_map/dot_general | solution.py:69
  21.8 29.7 %all-to-all-done = bf16[8,40,2048]{2,1,0:T(8,128)(2,1)} async-done(((bf16[8,40,2048]{2,1,0:T(8,128)(2,1)}), bf16[8,40,2048]{2,1,0:T(8,128)(2,1)}, u32[]{:S(2)}, u32[]{:S(2)}) %all-to-all-start) | async-done | bytes 1310752 | tf_op jit(solution)/shard_map/all_to_all | solution.py:84
  51.5 4.3 %all-to-all-start.1 = ((bf16[8,40,2048]{2,1,0:T(8,128)(2,1)}), bf16[8,40,2048]{2,1,0:T(8,128)(2,1)}, u32[]{:S(2)}, u32[]{:S(2)}) async-start(bf16[8,40,2048]{2,1,0:T(8,128)(2,1)} %bitcast.40), calls=%async_computation.1 | async-start | bytes 2621440 | tf_op jit(solution)/shard_map/all_to_all | solution.py:85
  55.8 5.4 %fusion = f32[320,1536]{1,0:T(8,128)S(1)} fusion(bf16[320,2048]{1,0:T(8,128)(2,1)} %bitcast.3, bf16[1,2048,1536]{2,1,0:T(8,128)(2,1)} %param.10), kind=kOutput, calls=%fused_computation.1 | convolution fusion | flops 2013265920 | bytes 9568256 | tf_op jit(solution)/shard_map/dot_general | solution.py:18
  61.2 0.0 copy-start.1
  61.2 1.3 copy-done.1
  62.5 1.1 multiply_convert_fusion.5
  63.6 24.5 %all-to-all-done.1 = bf16[8,40,2048]{2,1,0:T(8,128)(2,1)} async-done(((bf16[8,40,2048]{2,1,0:T(8,128)(2,1)}), bf16[8,40,2048]{2,1,0:T(8,128)(2,1)}, u32[]{:S(2)}, u32[]{:S(2)}) %all-to-all-start.1) | async-done | bytes 1310752 | tf_op jit(solution)/shard_map/all_to_all | solution.py:85
  88.0 0.0 copy-done
  88.0 0.0 copy-start.3
  88.0 2.8 %fusion.9 = f32[320]{0:T(512)S(1)} fusion(bf16[320,768]{1,0:T(8,128)(2,1)} %multiply_convert_fusion.5, bf16[1,768,2048]{2,1,0:T(8,128)(2,1)S(1)} %copy-done, bf16[320,2048]{1,0:T(8,128)(2,1)} %bitcast.28), kind=kOutput, calls=%fused_computation.13 | convolution fusion | flops 1008598720 | bytes 4949248 | tf_op jit(solution)/shard_map/dot_general | solution.py:28
  90.8 0.7 all_to_all.18
  91.5 3.3 %all-to-all-start.2 = ((f32[8,1,40]{2,1,0:T(1,128)}), f32[8,1,40]{2,1,0:T(1,128)S(1)}, u32[]{:S(2)}, u32[]{:S(2)}) async-start(f32[8,1,40]{2,1,0:T(1,128)} %all_to_all.18), calls=%async_computation.2 | async-start | bytes 8192 | tf_op jit(solution)/shard_map/all_to_all | solution.py:99
  94.8 0.0 reduce-scatter.5.cloned.1.call-start
  94.9 0.0 copy-done.3
  94.9 0.1 copy.40
  95.0 0.1 broadcast_in_dim.41
  95.1 5.1 %all-to-all-done.2 = f32[8,1,40]{2,1,0:T(1,128)S(1)} async-done(((f32[8,1,40]{2,1,0:T(1,128)}), f32[8,1,40]{2,1,0:T(1,128)S(1)}, u32[]{:S(2)}, u32[]{:S(2)}) %all-to-all-start.2) | async-done | bytes 1312 | tf_op jit(solution)/shard_map/all_to_all | solution.py:99
  100.2 0.5 broadcast.40
  100.7 0.7 reduce.9
  101.4 0.1 broadcast_in_dim.38
  101.5 0.2 select_reduce_fusion
  101.7 0.1 convert_element_type.99
  101.8 7.9 %all_to_all.25 = bf16[8,1,40]{2,1,0:T(2,128)(2,1)S(1)} all-to-all(bf16[8,1,40]{2,1,0:T(2,128)(2,1)S(1)} %convert_element_type.99), channel_id=1, replica_groups=mesh['dp'=4,'expert'=8] {'expert'}, dimensions={0} | all-to-all | bytes 1280 | tf_op jit(solution)/shard_map/all_to_all | solution.py:86
  109.7 0.1 reshape.101
  109.8 5.1 %convolution_convert_fusion.1 = bf16[768,2048]{1,0:T(8,128)(2,1)} fusion(bf16[320,768]{1,0:T(8,128)(2,1)} %multiply_convert_fusion.5, f32[320]{0:T(512)S(1)} %reshape.101, bf16[320,2048]{1,0:T(8,128)(2,1)} %bitcast.28), kind=kOutput, calls=%fused_computation.3 | convolution fusion | flops 1010171904 | bytes 4949248 | tf_op jit(solution)/shard_map/dot_general | solution.py:32
  114.9 0.0 reduce-scatter.5.cloned.1.call-update
  114.9 0.0 reduce-scatter.3.cloned.1.call-start
  115.0 0.0 copy-start.2
  115.0 1.7 multiply_convert_fusion.1
  116.7 0.2 copy-done.2
  116.9 1.6 multiply_convert_fusion.4
  118.5 6.9 %convolution_convert_fusion = bf16[2048,1536]{1,0:T(8,128)(2,1)} fusion(bf16[320,2048]{1,0:T(8,128)(2,1)} %bitcast.3, bf16[320,768]{1,0:T(8,128)(2,1)S(1)} %get-tuple-element.21, bf16[320,768]{1,0:T(8,128)(2,1)S(1)} %get-tuple-element.20), kind=kOutput, calls=%fused_computation | convolution fusion | flops 2018377728 | bytes 8585216 | tf_op jit(solution)/shard_map/dot_general | solution.py:44
  125.4 0.0 reduce-scatter.3.cloned.1.call-update
  125.4 0.1 reshape.98
  125.5 0.6 copy.42
  126.2 31.1 %reduce-scatter.5.cloned.1.call-done = bf16[768,512]{1,0:T(8,128)(2,1)} async-done(((bf16[768,2048]{1,0:T(8,128)(2,1)}), bf16[768,512]{1,0:T(8,128)(2,1)}) %reduce-scatter.5.cloned.1.call-update) | async-done | bytes 786448 | tf_op jit(solution)/shard_map/reduce_scatter | solution.py:109
  157.2 73.7 %reduce-scatter.3.cloned.1.call-done = bf16[512,1536]{1,0:T(8,128)(2,1)} async-done(((bf16[2048,1536]{1,0:T(8,128)(2,1)}), bf16[512,1536]{1,0:T(8,128)(2,1)}) %reduce-scatter.3.cloned.1.call-update) | async-done | bytes 1572880 | tf_op jit(solution)/shard_map/reduce_scatter | solution.py:106
  (7 shorter events, 0.1 us)
Async XLA Ops:
  7.2 80.9 %copy-start = (bf16[1,768,2048]{2,1,0:T(8,128)(2,1)S(1)}, bf16[1,768,2048]{2,1,0:T(8,128)(2,1)}, u32[]{:S(2)}) copy-start(bf16[1,768,2048]{2,1,0:T(8,128)(2,1)} %param.11) | copy-start | bytes 9437188
  12.9 38.6 %all-to-all-start = ((bf16[8,40,2048]{2,1,0:T(8,128)(2,1)}), bf16[8,40,2048]{2,1,0:T(8,128)(2,1)}, u32[]{:S(2)}, u32[]{:S(2)}) async-start(bf16[8,40,2048]{2,1,0:T(8,128)(2,1)} %bitcast.41), calls=%async_computation | async-start | bytes 2621440 | tf_op jit(solution)/shard_map/all_to_all | solution.py:84
  51.5 36.5 %all-to-all-start.1 = ((bf16[8,40,2048]{2,1,0:T(8,128)(2,1)}), bf16[8,40,2048]{2,1,0:T(8,128)(2,1)}, u32[]{:S(2)}, u32[]{:S(2)}) async-start(bf16[8,40,2048]{2,1,0:T(8,128)(2,1)} %bitcast.40), calls=%async_computation.1 | async-start | bytes 2621440 | tf_op jit(solution)/shard_map/all_to_all | solution.py:85
  61.2 1.3 copy-start.1
  88.0 6.8 %copy-start.3 = (f32[128,2]{0,1:T(2,128)S(1)}, f32[128,2]{0,1:T(2,128)}, u32[]{:S(2)}) copy-start(f32[128,2]{0,1:T(2,128)} %param.8) | copy-start | bytes 3076
  91.5 8.7 %all-to-all-start.2 = ((f32[8,1,40]{2,1,0:T(1,128)}), f32[8,1,40]{2,1,0:T(1,128)S(1)}, u32[]{:S(2)}, u32[]{:S(2)}) async-start(f32[8,1,40]{2,1,0:T(1,128)} %all_to_all.18), calls=%async_computation.2 | async-start | bytes 8192 | tf_op jit(solution)/shard_map/all_to_all | solution.py:99
  94.8 62.4 %reduce-scatter.5.cloned.1.call-start = ((), (), s32[]{:S(2)}) async-start(), calls=%async_computation.7 | async-start | bytes 3932160 | tf_op jit(solution)/shard_map/reduce_scatter | solution.py:109
  114.9 116.1 %reduce-scatter.3.cloned.1.call-start = ((), (), s32[]{:S(2)}) async-start(), calls=%async_computation.6 | async-start | bytes 7864320 | tf_op jit(solution)/shard_map/reduce_scatter | solution.py:106
  115.0 1.9 copy-start.2
Sparse Core Ops, SparseCore 0:
  115.0 42.1 reduce-scatter.4
  160.8 70.1 reduce-scatter.2
where the time goes:
time: 238 us
  waiting for transfers between devices  164 us (69%)
  matrix products  26.9 us (11%)
  between operations  14.2 us (6%)
  starting transfers between devices  14 us (6%)
  blocking collectives  7.92 us (3%)
  local copies, waits for them, and re-layouts  5.57 us (2%)
  other arithmetic  5.18 us (2%)
    reduce_scatter x1, waiting for transfers between devices, body(): lax.psum_scatter(grad_gu.astype(jnp.bfloat16), 'dp', scatter_dimension=0,...  73.7 us
    reduce_scatter x1, waiting for transfers between devices, body(): lax.psum_scatter(grad_down.astype(jnp.bfloat16), 'dp', scatter_dimension=...  31.1 us
    all_to_all x1, waiting for transfers between devices, body(): lax.all_to_all(send_x, 'expert', split_axis=0, concat_axis=0, tiled=True)  29.7 us
    all_to_all x1, waiting for transfers between devices, body(): lax.all_to_all(send_dy, 'expert', split_axis=0, concat_axis=0, tiled=True)  24.5 us
    all_to_all x1, blocking collectives, body(): lax.all_to_all(send_own.astype(jnp.bfloat16), 'expert', split_axis=0, con...  7.92 us
    dot_general x1, matrix products, backward_part(): lax.dot_general(rows_x, grad_both, (((0,), (0,)), ((), ())), preferred_el...  6.87 us
    all_to_all x1, starting transfers between devices, body(): lax.all_to_all(send_x, 'expert', split_axis=0, concat_axis=0, tiled=True)  6.33 us
    dot_general x1, matrix products, forward_part(): both_pre = jnp.dot(rows_x, weight_gu, preferred_element_type=jnp.float32)  5.38 us
  transfers between devices with their start and end apart: 5, of which 5 were waited for; matrix products, arithmetic and copies ran while one was open for 9% of the time, Pallas kernels for 0%

commit v1 on v0

v1 whole, which is shorter than its diff:
```python
import functools

import jax
import jax.numpy as jnp
from jax import lax
from jax.experimental import pallas as pl
from jax.experimental.pallas import tpu as pltpu
from jax.sharding import PartitionSpec as P

EXPERTS = 8
CAP = 40
VMEM_LIMIT = 56 * 1024 * 1024
BF16 = jnp.bfloat16
F32 = jnp.float32


def dispatch_kernel(ids_ref, probs_ref, x_ref, dy_ref, *outs):
    row_refs, slot_ref = outs[:-1], outs[-1]
    me = lax.axis_index("expert")
    tok = x_ref.shape[0]
    width = x_ref.shape[1]
    numbers = lax.broadcasted_iota(jnp.int32, (EXPERTS, tok), 0)
    first = jnp.bitwise_xor(ids_ref[0:1, :], me) == numbers
    second = jnp.bitwise_xor(ids_ref[1:2, :], me) == numbers
    either = jnp.where(first | second, 1.0, 0.0)
    prob = jnp.where(first, probs_ref[0:1, :], 0.0) + jnp.where(second, probs_ref[1:2, :], 0.0)
    before = jnp.where(
        lax.broadcasted_iota(jnp.int32, (tok, tok), 0)
        < lax.broadcasted_iota(jnp.int32, (tok, tok), 1),
        1.0,
        0.0,
    )
    position = jnp.dot(either.astype(BF16), before.astype(BF16), preferred_element_type=F32)
    slot = position.astype(jnp.int32) + numbers * CAP
    slot_ref[0:1, :] = jnp.sum(jnp.where(first, slot, 0), axis=0, keepdims=True)
    slot_ref[1:2, :] = jnp.sum(jnp.where(second, slot, 0), axis=0, keepdims=True)
    target = jnp.where(either > 0.5, position, -1.0)
    places = lax.broadcasted_iota(jnp.int32, (CAP, tok), 0).astype(F32)
    picks = [
        jnp.where(places == target[e : e + 1, :], 1.0, 0.0) for e in range(EXPERTS)
    ]
    row_prob = [
        jnp.sum(picks[e] * prob[e : e + 1, :], axis=1, keepdims=True) for e in range(EXPERTS)
    ]
    pick = jnp.concatenate(picks, axis=0).astype(BF16)
    step = 512
    for at in range(0, width, step):
        rows_x = jnp.dot(pick, x_ref[:, at : at + step], preferred_element_type=F32)
        rows_dy = jnp.dot(pick, dy_ref[:, at : at + step], preferred_element_type=F32)
        for e in range(EXPERTS):
            part = slice(e * CAP, (e + 1) * CAP)
            row_refs[e][:, at : at + step] = rows_x[part].astype(BF16)
            row_refs[e][:, width + at : width + at + step] = (row_prob[e] * rows_dy[part]).astype(
                BF16
            )


def dispatch_rows(ids, probs, tokens, cotangent):
    tok, width = tokens.shape
    return pl.pallas_call(
        dispatch_kernel,
        out_shape=[jax.ShapeDtypeStruct((CAP, 2 * width), BF16)] * EXPERTS
        + [jax.ShapeDtypeStruct((2, tok), jnp.int32)],
        compiler_params=pltpu.CompilerParams(vmem_limit_bytes=VMEM_LIMIT),
        cost_estimate=pl.CostEstimate(
            flops=4 * EXPERTS * CAP * tok * width, bytes_accessed=4_000_000, transcendentals=0
        ),
        name="dispatch_rows",
    )(ids, probs, tokens, cotangent)


def expert_kernel(a_ref, b_ref, gate_ref, up_ref, down_ref, *rest):
    groups = len(rest) - 4
    message_refs, inner_ref, x_rows, s_rows, total = rest[:groups], *rest[groups:]
    width = gate_ref.shape[0]
    tile = gate_ref.shape[1]
    half = tile * pl.num_programs(0)
    quarter = width // groups
    factors = message_refs[0].shape[1] - 2 * quarter
    step = pl.program_id(0)
    group = lax.axis_index("dp")

    @pl.when(step == 0)
    def _():
        for rows, start in ((x_rows, 0), (s_rows, width)):
            rows[...] = jnp.concatenate(
                [
                    a_ref[:, start : start + width].astype(F32),
                    b_ref[:, start : start + width].astype(F32),
                ],
                axis=0,
            ).astype(BF16)
        for m in range(groups):
            at = pl.multiple_of(jnp.bitwise_xor(group, m) * quarter, quarter)
            message_refs[m][:, factors : factors + quarter] = x_rows[:, pl.ds(at, quarter)]
            message_refs[m][:, factors + quarter :] = s_rows[:, pl.ds(at, quarter)]
        total[...] = jnp.zeros_like(total)

    x, s = x_rows[...], s_rows[...]
    gate = jnp.dot(x, gate_ref[...], preferred_element_type=F32)
    up = jnp.dot(x, up_ref[...], preferred_element_type=F32)
    grad_hidden = lax.dot_general(
        s, down_ref[...], (((1,), (1,)), ((), ())), preferred_element_type=F32
    )
    sigmoid = 1.0 / (1.0 + jnp.exp(-gate))
    activated = gate * sigmoid
    hidden = (activated * up).astype(BF16)
    grad_gate = (grad_hidden * up * sigmoid * (1.0 + gate * (1.0 - sigmoid))).astype(BF16)
    grad_up = (grad_hidden * activated).astype(BF16)
    total[...] += jnp.sum(hidden.astype(F32) * grad_hidden, axis=1, keepdims=True)
    for part, values in enumerate((grad_gate, grad_up, hidden)):
        at = pl.multiple_of(part * half + step * tile, tile)
        for message in message_refs:
            message[:, pl.ds(at, tile)] = values

    @pl.when(step == pl.num_programs(0) - 1)
    def _():
        inner_ref[...] = total[...]


def expert_rows(rows_a, rows_b, weight_gu, weight_down, groups):
    width, both = weight_gu.shape
    half = both // 2
    tile = 256
    steps = half // tile
    count = 2 * CAP
    message = jax.ShapeDtypeStruct((count, 3 * half + 2 * (width // groups)), BF16)

    def whole(shape):
        return pl.BlockSpec(shape, lambda h: (0, 0))

    return pl.pallas_call(
        expert_kernel,
        grid=(steps,),
        in_specs=[
            whole(rows_a.shape),
            whole(rows_b.shape),
            pl.BlockSpec((width, tile), lambda h: (0, h)),
            pl.BlockSpec((width, tile), lambda h: (0, h + steps)),
            pl.BlockSpec((tile, width), lambda h: (h, 0)),
        ],
        out_specs=[whole(message.shape)] * groups + [whole((count, 1))],
        out_shape=[message] * groups + [jax.ShapeDtypeStruct((count, 1), F32)],
        scratch_shapes=[
            pltpu.VMEM((count, width), BF16),
            pltpu.VMEM((count, width), BF16),
            pltpu.VMEM((count, 1), F32),
        ],
        compiler_params=pltpu.CompilerParams(vmem_limit_bytes=VMEM_LIMIT),
        cost_estimate=pl.CostEstimate(
            flops=2 * 256 * width * 3 * half * 2,
            bytes_accessed=2 * width * 3 * half,
            transcendentals=count * half,
        ),
        name="expert_rows",
    )(rows_a, rows_b, weight_gu, weight_gu, weight_down)


def gradient_kernel(pieces, half, final, *refs):
    piece_refs = refs[:pieces]
    if final:
        acc_gu, acc_down, out_gu, out_down, rows, turned, sems = refs[pieces:]
    else:
        out_gu, out_down, rows, turned, sems = refs[pieces:]
    count = piece_refs[0].shape[0]
    quarter = out_gu.shape[0]
    copies = [
        pltpu.make_async_copy(ref, rows.at[pl.ds(n * count, count), :], sems.at[n])
        for n, ref in enumerate(piece_refs)
    ]
    for copy in copies:
        copy.start()
    for copy in copies:
        copy.wait()
    factors = 3 * half
    tile = 256
    turned[...] = rows[:, factors : factors + quarter].T
    for at in range(0, 2 * half, tile):
        grad = jnp.dot(turned[...], rows[:, at : at + tile], preferred_element_type=F32)
        if final:
            grad = grad + acc_gu[:, at : at + tile]
        out_gu[:, at : at + tile] = grad.astype(out_gu.dtype)
    for at in range(0, half, tile):
        grad = jnp.dot(
            rows[:, 2 * half + at : 2 * half + at + tile].T,
            rows[:, factors + quarter :],
            preferred_element_type=F32,
        )
        if final:
            grad = grad + acc_down[at : at + tile, :]
        out_down[at : at + tile, :] = grad.astype(out_down.dtype)


def gradients(pieces, half, quarter, sums=None):
    final = sums is not None
    kept = BF16 if final else F32
    count, message = pieces[0].shape
    rows = count * len(pieces)
    vmem = pl.BlockSpec(memory_space=pltpu.VMEM)
    return pl.pallas_call(
        functools.partial(gradient_kernel, len(pieces), half, final),
        in_specs=[pl.BlockSpec(memory_space=pl.ANY)] * len(pieces) + ([vmem] * 2 if final else []),
        out_specs=[vmem] * 2,
        out_shape=[
            jax.ShapeDtypeStruct((quarter, 2 * half), kept),
            jax.ShapeDtypeStruct((half, quarter), kept),
        ],
        scratch_shapes=[
            pltpu.VMEM((rows, message), BF16),
            pltpu.VMEM((quarter, rows), BF16),
            pltpu.SemaphoreType.DMA((len(pieces),)),
        ],
        compiler_params=pltpu.CompilerParams(vmem_limit_bytes=VMEM_LIMIT),
        cost_estimate=pl.CostEstimate(
            flops=2 * rows * quarter * 3 * half,
            bytes_accessed=2 * rows * message,
            transcendentals=0,
        ),
        name="gradients",
    )(*pieces, *(sums or ()))


def exchange(values, axis, mask):
    size = lax.axis_size(axis)
    return lax.ppermute(values, axis, [(n, n ^ mask) for n in range(size)])


def plane_body(tokens, cotangent, gate_probs, expert_ids, gate_up, down):
    groups = lax.axis_size("dp")
    me = lax.axis_index("expert")
    half = gate_up.shape[2] // 2
    quarter = tokens.shape[1] // groups
    ids, probs = expert_ids.T, gate_probs.T
    *local, slots = dispatch_rows(ids, probs, tokens, cotangent)
    arrived = [local[0]] + [exchange(local[k], "expert", k) for k in range(1, EXPERTS)]
    pieces, inner = [], []
    for chunk in range(EXPERTS // 2):
        *messages, chunk_inner = expert_rows(
            arrived[2 * chunk], arrived[2 * chunk + 1], gate_up[0], down[0], groups
        )
        inner.append(chunk_inner.reshape(-1))
        pieces.append(
            [messages[0]] + [exchange(messages[m], "dp", m) for m in range(1, groups)]
        )
    early = [piece for chunk in pieces[:-1] for piece in chunk]
    sums = gradients(early, half, quarter)
    grad_gu, grad_down = gradients(pieces[-1], half, quarter, tuple(sums))
    gathered = lax.all_gather(jnp.concatenate(inner), "expert").reshape(EXPERTS, EXPERTS, CAP)
    numbers = jnp.arange(EXPERTS, dtype=jnp.int32)
    mine = numbers[:, None] == jnp.bitwise_xor(numbers, me)[None, :]
    returned = jnp.sum(jnp.where(mine[:, :, None], gathered, 0.0), axis=0).reshape(-1)
    chosen = slots[:, None, :] == jnp.arange(EXPERTS * CAP, dtype=jnp.int32)[None, :, None]
    grad_probs = jnp.sum(jnp.where(chosen, returned[None, :, None], 0.0), axis=1) / probs
    return (grad_probs.T, grad_gu[None], grad_down[None])


def widen(values, slices, expert_count):
    tail = values.shape[1:]
    spread = values.reshape((EXPERTS, 1, CAP) + tail)
    spread = jnp.broadcast_to(spread, (EXPERTS, slices, CAP) + tail)
    return spread.reshape((expert_count, CAP) + tail)


def swap(values):
    return lax.all_to_all(values, "expert", split_axis=0, concat_axis=0, tiled=True)


def sliced_body(tokens, cotangent, gate_probs, expert_ids, gate_up, down):
    expert_count = lax.axis_size("expert")
    slices = expert_count // EXPERTS
    tok_count, width = tokens.shape
    choose_count = expert_ids.shape[1]
    half = gate_up.shape[2] // 2
    slot_rows = EXPERTS * CAP
    flat_ids = expert_ids.reshape(-1)
    choose = (flat_ids[:, None] == jnp.arange(EXPERTS, dtype=jnp.int32)[None, :]).astype(jnp.int32)
    earlier = jnp.cumsum(choose, axis=0) - choose
    slot_of = flat_ids * CAP + jnp.sum(earlier * choose, axis=1)
    picked = jnp.arange(slot_rows, dtype=jnp.int32)[:, None] == slot_of[None, :]
    picked_tok = jnp.any(picked.reshape(slot_rows, tok_count, choose_count), axis=2).astype(BF16)
    slot_prob = jnp.sum(jnp.where(picked, gate_probs.reshape(-1)[None, :], 0.0), axis=1)
    local_x = jnp.dot(picked_tok, tokens, preferred_element_type=F32).astype(BF16)
    local_dy = jnp.dot(picked_tok, cotangent, preferred_element_type=F32)
    local_scaled = (slot_prob[:, None] * local_dy).astype(BF16)
    rows_x = swap(widen(local_x, slices, expert_count)).reshape(-1, width)
    rows_s = swap(widen(local_scaled, slices, expert_count)).reshape(-1, width)
    both = jnp.dot(rows_x, gate_up[0], preferred_element_type=F32)
    gate, up = both[:, :half], both[:, half:]
    sigmoid = jax.nn.sigmoid(gate)
    activated = gate * sigmoid
    hidden = (activated * up).astype(BF16)
    grad_hidden = lax.dot_general(
        rows_s, down[0], (((1,), (1,)), ((), ())), preferred_element_type=F32
    )
    inner = jnp.sum(hidden.astype(F32) * grad_hidden, axis=1)
    grad_gate = (grad_hidden * up * sigmoid * (1.0 + gate * (1.0 - sigmoid))).astype(BF16)
    grad_up = (grad_hidden * activated).astype(BF16)
    grad_both = jnp.concatenate([grad_gate, grad_up], axis=1)
    over_rows = (((0,), (0,)), ((), ()))
    grad_gu = lax.dot_general(rows_x, grad_both, over_rows, preferred_element_type=F32)
    grad_down = lax.dot_general(hidden, rows_s, over_rows, preferred_element_type=F32)
    returned = swap(inner.reshape(expert_count, CAP))
    per_slot = jnp.sum(returned.reshape(EXPERTS, slices, CAP), axis=1).reshape(slot_rows)
    grad_probs = jnp.sum(jnp.where(picked, per_slot[:, None], 0.0), axis=0)
    grad_probs = grad_probs.reshape(tok_count, choose_count) / gate_probs
    reduced_gu = lax.psum_scatter(grad_gu.astype(BF16), "dp", scatter_dimension=0, tiled=True)
    reduced_down = lax.psum_scatter(grad_down.astype(BF16), "dp", scatter_dimension=1, tiled=True)
    return (grad_probs, reduced_gu[None], reduced_down[None])


def solution(mesh):
    whole_experts = mesh.shape["expert"] == EXPERTS and mesh.shape["dp"] == 4
    return jax.shard_map(
        plane_body if whole_experts else sliced_body,
        mesh=mesh,
        in_specs=(
            P(("dp", "expert"), None),
            P(("dp", "expert"), None),
            P(("dp", "expert"), None),
            P(("dp", "expert"), None),
            P("expert", None, None),
            P("expert", None, None),
        ),
        out_specs=(P(("dp", "expert"), None), P("expert", "dp", None), P("expert", None, "dp")),
        check_vma=False,
    )
```

time: 238 us -> 156 us (0.66)
  waiting for transfers between devices: 164 us -> 49.1 us
  Pallas kernels: 0 us -> 46.9 us
  matrix products: 26.9 us -> 0 us
  blocking collectives: 7.92 us -> 26.9 us
  between operations: 14.2 us -> 1.38 us
  starting transfers between devices: 14 us -> 25.6 us
  local copies, waits for them, and re-layouts: 5.57 us -> 2.53 us
    reduce_scatter x2 -> x0, waiting for transfers between devices: 105 us -> none  [the longest x1 73.7 us: body(): lax.psum_scatter(grad_gu.astype(jnp.bfloat16), 'dp', scatter_dimension=0,...]
    all_to_all x3 -> x0, waiting for transfers between devices: 59.3 us -> none  [the longest x1 29.7 us: body(): lax.all_to_all(send_x, 'expert', split_axis=0, concat_axis=0, tiled=True)]
    ppermute x0 -> x19, waiting for transfers between devices: none -> 49.1 us  [exchange(): return lax.ppermute(values, axis, [(n, n ^ mask) for n in range(size)])]
    pallas_call x0 -> x7, Pallas kernels: none -> 46.9 us  [the longest x4 30.1 us: expert_rows(): pl.pallas_call(expert_kernel, grid=(steps,), in_specs=[whole(rows_a.shape...]
    unnamed x0 -> x1, blocking collectives: none -> 26.9 us
    dot_general x7 -> x0, matrix products: 26.9 us -> none  [the longest x1 6.87 us: backward_part(): lax.dot_general(rows_x, grad_both, (((0,), (0,)), ((), ())), preferred_el...]
    ppermute x0 -> x19, starting transfers between devices: none -> 25.6 us  [exchange(): return lax.ppermute(values, axis, [(n, n ^ mask) for n in range(size)])]
    all_to_all x3 -> x0, starting transfers between devices: 13.9 us -> none  [the longest x1 6.33 us: body(): lax.all_to_all(send_x, 'expert', split_axis=0, concat_axis=0, tiled=True)]
  transfers between devices with their start and end apart: 5 -> 19, of which waited for: 5 -> 7; matrix products, arithmetic and copies ran while one was open for 9% -> 3% of each run, Pallas kernels for 0% -> 24%
where the time goes in v1:
time: 156 us; the launch traced here: 155 us
  waiting for transfers between devices  49.1 us (31%)
  Pallas kernels  46.9 us (30%)
  blocking collectives  26.9 us (17%)
  starting transfers between devices  25.6 us (16%)
  other arithmetic  2.88 us (2%)
  local copies, waits for them, and re-layouts  2.53 us (2%)
    ppermute x19, waiting for transfers between devices, exchange(): return lax.ppermute(values, axis, [(n, n ^ mask) for n in range(size)])  49.1 us
    pallas_call x4, Pallas kernels, expert_rows(): pl.pallas_call(expert_kernel, grid=(steps,), in_specs=[whole(rows_a.shape...  30.1 us
    unnamed x1, blocking collectives  26.9 us
    ppermute x19, starting transfers between devices, exchange(): return lax.ppermute(values, axis, [(n, n ^ mask) for n in range(size)])  25.6 us
    pallas_call x2, Pallas kernels, gradients(): pl.pallas_call(functools.partial(gradient_kernel, len(pieces), half, fina...  13.2 us
    pallas_call x1, Pallas kernels, dispatch_rows(): pl.pallas_call(dispatch_kernel, out_shape=[jax.ShapeDtypeStruct((CAP, 2 *...  3.59 us
  transfers between devices with their start and end apart: 19, of which 7 were waited for; matrix products, arithmetic and copies ran while one was open for 3% of the time, Pallas kernels for 24%

profile of v1, /device:TPU:0, one launch (start us, length us, event | category | flops | bytes accessed | tf_op | source)
XLA Modules:
  0.0 155.3 jit_solution(16591454905344307534)
XLA Ops:
  0.6 3.6 %dispatch_rows.1 = (bf16[40,4096]{1,0:T(8,128)(2,1)}, bf16[40,4096]{1,0:T(8,128)(2,1)}, bf16[40,4096]{1,0:T(8,128)(2,1)}, bf16[40,4096]{1,0:T(8,128)(2,1)}, bf16...) custom-call(s32[2,128]{1,0:T(2,128)} %bitcast.24, ...), custom_call_target="tpu_custom_call" | custom-call | flops 335544320 | bytes 4000000 | tf_op jit(solution)/shard_map/dispatch_rows/pallas_call | solution.py:60
  4.2 3.0 %collective-permute-start.1 = (bf16[40,4096]{1,0:T(8,128)(2,1)}, bf16[40,4096]{1,0:T(8,128)(2,1)S(1)}, u32[]{:S(2)}, u32[]{:S(2)}) collective-permute-start(bf16[40,4096]{1,0:T(8,128)(2,1)} %get-tuple-element.40), channel_id=1, source_target_pairs={{0,2},{1,3},{2,0},{3,1},{4,6},{5,7},{6,4},{7,5},{8,10},{9,11},{10,... | collective-permute-start | bytes 983048 | tf_op jit(solution)/shard_map/ppermute | solution.py:225
  7.2 0.0 collective-permute-start.2
  7.2 2.6 %collective-permute-start.3 = (bf16[40,4096]{1,0:T(8,128)(2,1)}, bf16[40,4096]{1,0:T(8,128)(2,1)S(1)}, u32[]{:S(2)}, u32[]{:S(2)}) collective-permute-start(bf16[40,4096]{1,0:T(8,128)(2,1)} %get-tuple-element.43), channel_id=1, source_target_pairs={{0,4},{1,5},{2,6},{3,7},{4,0},{5,1},{6,2},{7,3},{8,12},{9,13},{10,... | collective-permute-start | bytes 983048 | tf_op jit(solution)/shard_map/ppermute | solution.py:225
  9.8 0.2 collective-permute-start.4
  10.0 0.3 collective-permute-start
  10.3 0.1 broadcast_in_dim.37
  10.4 0.1 broadcast_in_dim.38
  10.5 1.2 dynamic-slice
  12.2 16.7 %collective-permute-done.1.a_ref = bf16[40,4096]{1,0:T(8,128)(2,1)S(1)} collective-permute-done((bf16[40,4096]{1,0:T(8,128)(2,1)}, bf16[40,4096]{1,0:T(8,128)(2,1)S(1)}, u32[]{:S(2)}, u32[]{:S(2)}) %collective-permute-start.1) | collective-permute-done | bytes 327712 | tf_op jit(solution)/shard_map/ppermute | solution.py:225
  29.0 1.8 %collective-permute-start.5 = (bf16[40,4096]{1,0:T(8,128)(2,1)}, bf16[40,4096]{1,0:T(8,128)(2,1)S(1)}, u32[]{:S(2)}, u32[]{:S(2)}) collective-permute-start(bf16[40,4096]{1,0:T(8,128)(2,1)} %get-tuple-element.46), channel_id=1, source_target_pairs={{0,6},{1,7},{2,4},{3,5},{4,2},{5,3},{6,0},{7,1},{8,14},{9,15},{10,... | collective-permute-start | bytes 983048 | tf_op jit(solution)/shard_map/ppermute | solution.py:225
  30.8 3.6 %collective-permute-done.2.b_ref = bf16[40,4096]{1,0:T(8,128)(2,1)S(1)} collective-permute-done((bf16[40,4096]{1,0:T(8,128)(2,1)}, bf16[40,4096]{1,0:T(8,128)(2,1)S(1)}, u32[]{:S(2)}, u32[]{:S(2)}) %collective-permute-start.2) | collective-permute-done | bytes 327712 | tf_op jit(solution)/shard_map/ppermute | solution.py:225
  34.3 2.0 %collective-permute-start.6 = (bf16[40,4096]{1,0:T(8,128)(2,1)}, bf16[40,4096]{1,0:T(8,128)(2,1)S(1)}, u32[]{:S(2)}, u32[]{:S(2)}) collective-permute-start(bf16[40,4096]{1,0:T(8,128)(2,1)} %get-tuple-element.47), channel_id=1, source_target_pairs={{0,7},{1,6},{2,5},{3,4},{4,3},{5,2},{6,1},{7,0},{8,15},{9,14},{10,... | collective-permute-start | bytes 983048 | tf_op jit(solution)/shard_map/ppermute | solution.py:225
  36.4 0.0 copy-done.18
  36.4 7.5 %expert_rows.5 = (bf16[80,3328]{1,0:T(8,128)(2,1)}, bf16[80,3328]{1,0:T(8,128)(2,1)}, bf16[80,3328]{1,0:T(8,128)(2,1)}, bf16[80,3328]{1,0:T(8,128)(2,1)}, f32[80,1]{1,0:T(8,128)}) custom-call(bf16[40,4096]{1,0:T(8,128)(2,1)} %copy-done.18, bf16[40,4096]{1,0:T(8,128)(2,1)} %copy-done.19, bf16[2048,1536]{1,0:T(8,128)(2,1)} %bitcast.10, ...), custom_call_target="tpu_custom_call" | custom-call | flops 4831838208 | bytes 9437184 | tf_op jit(solution)/shard_map/expert_rows/pallas_call | solution.py:132
  43.9 0.0 collective-permute-done.3.a_ref
  43.9 1.5 collective-permute-start.13
  45.4 7.8 %collective-permute-done.4.b_ref = bf16[40,4096]{1,0:T(8,128)(2,1)S(1)} collective-permute-done((bf16[40,4096]{1,0:T(8,128)(2,1)}, bf16[40,4096]{1,0:T(8,128)(2,1)S(1)}, u32[]{:S(2)}, u32[]{:S(2)}) %collective-permute-start.4) | collective-permute-done | bytes 327712 | tf_op jit(solution)/shard_map/ppermute | solution.py:225
  53.3 1.6 %collective-permute-start.14 = (bf16[80,3328]{1,0:T(8,128)(2,1)}, bf16[80,3328]{1,0:T(8,128)(2,1)S(1)}, u32[]{:S(2)}, u32[]{:S(2)}) collective-permute-start(bf16[80,3328]{1,0:T(8,128)(2,1)} %get-tuple-element.59), channel_id=1, source_target_pairs={{0,16},{8,24},{16,0},{24,8},{1,17},{9,25},{17,1},{25,9},{2,18},{10... | collective-permute-start | bytes 1597448 | tf_op jit(solution)/shard_map/ppermute | solution.py:225
  54.9 0.0 copy-done.16
  54.9 7.5 %expert_rows.6 = (bf16[80,3328]{1,0:T(8,128)(2,1)}, bf16[80,3328]{1,0:T(8,128)(2,1)}, bf16[80,3328]{1,0:T(8,128)(2,1)}, bf16[80,3328]{1,0:T(8,128)(2,1)}, f32[80,1]{1,0:T(8,128)}) custom-call(bf16[40,4096]{1,0:T(8,128)(2,1)} %copy-done.16, bf16[40,4096]{1,0:T(8,128)(2,1)} %copy-done.17, bf16[2048,1536]{1,0:T(8,128)(2,1)} %bitcast.12, ...), custom_call_target="tpu_custom_call" | custom-call | flops 4831838208 | bytes 9437184 | tf_op jit(solution)/shard_map/expert_rows/pallas_call | solution.py:132
  62.4 0.0 collective-permute-done.b_ref
  62.4 1.7 %collective-permute-start.15 = (bf16[80,3328]{1,0:T(8,128)(2,1)}, bf16[80,3328]{1,0:T(8,128)(2,1)S(1)}, u32[]{:S(2)}, u32[]{:S(2)}) collective-permute-start(bf16[80,3328]{1,0:T(8,128)(2,1)} %get-tuple-element.60), channel_id=1, source_target_pairs={{0,24},{8,16},{16,8},{24,0},{1,25},{9,17},{17,9},{25,1},{2,26},{10... | collective-permute-start | bytes 1597448 | tf_op jit(solution)/shard_map/ppermute | solution.py:225
  64.1 0.0 collective-permute-done.5.a_ref
  64.1 0.5 collective-permute-start.16
  64.7 7.6 %expert_rows.4 = (bf16[80,3328]{1,0:T(8,128)(2,1)}, bf16[80,3328]{1,0:T(8,128)(2,1)}, bf16[80,3328]{1,0:T(8,128)(2,1)}, bf16[80,3328]{1,0:T(8,128)(2,1)}, f32[80,1]{1,0:T(8,128)}) custom-call(bf16[40,4096]{1,0:T(8,128)(2,1)} %get-tuple-element.37.a_ref, bf16[40,4096]{1,0:T(8,128)(2,1)} %copy-done.14, bf16[2048,1536]{1,0:T(8,128)(2,1)} %bitcast.14, ...), custom_call_target="tpu_custom_call" | custom-call | flops 4831838208 | bytes 9437184 | tf_op jit(solution)/shard_map/expert_rows/pallas_call | solution.py:132
  72.2 0.0 copy-done.3
  72.3 0.1 reduce.2
  72.4 0.1 reduce.3
  72.5 0.9 reduce.1
  73.4 0.0 collective-permute-done.6.b_ref
  73.4 1.4 collective-permute-start.17
  74.8 0.0 collective-permute-done.13.refs_5_
  74.8 1.6 %collective-permute-start.18 = (bf16[80,3328]{1,0:T(8,128)(2,1)}, bf16[80,3328]{1,0:T(8,128)(2,1)}, u32[]{:S(2)}, u32[]{:S(2)}) collective-permute-start(bf16[80,3328]{1,0:T(8,128)(2,1)} %get-tuple-element.64), channel_id=1, source_target_pairs={{0,24},{8,16},{16,8},{24,0},{1,25},{9,17},{17,9},{25,1},{2,26},{10... | collective-permute-start | bytes 1597448 | tf_op jit(solution)/shard_map/ppermute | solution.py:225
  76.4 3.3 %collective-permute-done.14.refs_6_ = bf16[80,3328]{1,0:T(8,128)(2,1)S(1)} collective-permute-done((bf16[80,3328]{1,0:T(8,128)(2,1)}, bf16[80,3328]{1,0:T(8,128)(2,1)S(1)}, u32[]{:S(2)}, u32[]{:S(2)}) %collective-permute-start.14) | collective-permute-done | bytes 532512 | tf_op jit(solution)/shard_map/ppermute | solution.py:225
  79.8 0.0 copy-start.5
  79.8 1.7 %collective-permute-start.10 = (bf16[80,3328]{1,0:T(8,128)(2,1)}, bf16[80,3328]{1,0:T(8,128)(2,1)}, u32[]{:S(2)}, u32[]{:S(2)}) collective-permute-start(bf16[80,3328]{1,0:T(8,128)(2,1)} %get-tuple-element.54), channel_id=1, source_target_pairs={{0,8},{8,0},{16,24},{24,16},{1,9},{9,1},{17,25},{25,17},{2,10},{10... | collective-permute-start | bytes 1597448 | tf_op jit(solution)/shard_map/ppermute | solution.py:225
  81.5 7.5 %expert_rows.7 = (bf16[80,3328]{1,0:T(8,128)(2,1)}, bf16[80,3328]{1,0:T(8,128)(2,1)}, bf16[80,3328]{1,0:T(8,128)(2,1)}, bf16[80,3328]{1,0:T(8,128)(2,1)}, f32[80,1]{1,0:T(8,128)}) custom-call(bf16[40,4096]{1,0:T(8,128)(2,1)} %copy-done.13, bf16[40,4096]{1,0:T(8,128)(2,1)} %copy-done.15, bf16[2048,1536]{1,0:T(8,128)(2,1)} %bitcast.16, ...), custom_call_target="tpu_custom_call" | custom-call | flops 4831838208 | bytes 9437184 | tf_op jit(solution)/shard_map/expert_rows/pallas_call | solution.py:132
  89.0 0.9 reduce.4
  89.9 0.0 collective-permute-done.15.refs_7_
  89.9 1.6 %collective-permute-start.11 = (bf16[80,3328]{1,0:T(8,128)(2,1)}, bf16[80,3328]{1,0:T(8,128)(2,1)}, u32[]{:S(2)}, u32[]{:S(2)}) collective-permute-start(bf16[80,3328]{1,0:T(8,128)(2,1)} %get-tuple-element.55), channel_id=1, source_target_pairs={{0,16},{8,24},{16,0},{24,8},{1,17},{9,25},{17,1},{25,9},{2,18},{10... | collective-permute-start | bytes 1597448 | tf_op jit(solution)/shard_map/ppermute | solution.py:225
  91.5 0.0 collective-permute-done.16.refs_9_
  91.5 0.4 collective-permute-start.12
  91.9 0.2 maximum_dynamic-update-slice_fusion
  92.1 26.9 %all-reduce = f32[2560]{0:T(1024)S(1)} all-reduce(f32[2560]{0:T(1024)S(1)} %maximum_dynamic-update-slice_fusion), channel_id=2, replica_groups=mesh['dp'=4,'expert'=8] {'expert'}, use_global_device_ids=true, to_apply=%add | all-reduce | flops 2560 | bytes 20480
  119.0 0.1 reshape.51
  119.1 0.0 collective-permute-done.17.refs_10_
  119.1 0.0 copy-start.12
  119.1 1.5 collective-permute-start.7
  120.6 0.0 collective-permute-done.18.refs_11_
  120.6 1.7 %collective-permute-start.8 = (bf16[80,3328]{1,0:T(8,128)(2,1)}, bf16[80,3328]{1,0:T(8,128)(2,1)S(1)}, u32[]{:S(2)}, u32[]{:S(2)}) collective-permute-start(bf16[80,3328]{1,0:T(8,128)(2,1)} %get-tuple-element.51), channel_id=1, source_target_pairs={{0,16},{8,24},{16,0},{24,8},{1,17},{9,25},{17,1},{25,9},{2,18},{10... | collective-permute-start | bytes 1597448 | tf_op jit(solution)/shard_map/ppermute | solution.py:225
  122.3 0.0 collective-permute-done.10.refs_1_
  122.3 0.3 collective-permute-start.9
  122.7 0.1 select_reduce_fusion
  122.8 0.6 bitcast_divide_fusion
  123.4 2.1 %collective-permute-done.11.refs_2_ = bf16[80,3328]{1,0:T(8,128)(2,1)} collective-permute-done((bf16[80,3328]{1,0:T(8,128)(2,1)}, bf16[80,3328]{1,0:T(8,128)(2,1)}, u32[]{:S(2)}, u32[]{:S(2)}) %collective-permute-start.11) | collective-permute-done | bytes 532512 | tf_op jit(solution)/shard_map/ppermute | solution.py:225
  125.5 0.0 collective-permute-done.12.refs_3_
  125.5 6.9 %gradients.2 = (f32[512,1536]{1,0:T(8,128)}, f32[768,512]{1,0:T(8,128)}) custom-call(bf16[80,3328]{1,0:T(8,128)(2,1)} %get-tuple-element.53.refs_0_, bf16[80,3328]{1,0:T(8,128)(2,1)} %collective-permute-done.10.refs_1_, bf16[80,3328]{1,0:T(8,128)(2,1)} %collective-permute-done.11.refs_2_, bf16[80,3328]{1,0:T(8,128)(2,1)} %collective-permute-done.12.refs_3_, ...), custom_call_target="tpu_custom_call" | custom-call | flops 2264924160 | bytes 6389760 | tf_op jit(solution)/shard_map/gradients/pallas_call | solution.py:200
  132.4 2.5 %collective-permute-done.7.refs_1_ = bf16[80,3328]{1,0:T(8,128)(2,1)S(1)} collective-permute-done((bf16[80,3328]{1,0:T(8,128)(2,1)}, bf16[80,3328]{1,0:T(8,128)(2,1)S(1)}, u32[]{:S(2)}, u32[]{:S(2)}) %collective-permute-start.7) | collective-permute-done | bytes 532512 | tf_op jit(solution)/shard_map/ppermute | solution.py:225
  134.9 13.0 %collective-permute-done.8.refs_2_ = bf16[80,3328]{1,0:T(8,128)(2,1)S(1)} collective-permute-done((bf16[80,3328]{1,0:T(8,128)(2,1)}, bf16[80,3328]{1,0:T(8,128)(2,1)S(1)}, u32[]{:S(2)}, u32[]{:S(2)}) %collective-permute-start.8) | collective-permute-done | bytes 532512 | tf_op jit(solution)/shard_map/ppermute | solution.py:225
  147.9 0.0 collective-permute-done.9.refs_3_
  148.0 0.8 copy-done.1
  148.7 0.2 copy-done.2
  149.0 6.3 %gradients.3 = (bf16[512,1536]{1,0:T(8,128)(2,1)}, bf16[768,512]{1,0:T(8,128)(2,1)}) custom-call(bf16[80,3328]{1,0:T(8,128)(2,1)} %get-tuple-element.49.refs_0_, bf16[80,3328]{1,0:T(8,128)(2,1)} %copy-done, bf16[80,3328]{1,0:T(8,128)(2,1)} %copy-done.1, bf16[80,3328]{1,0:T(8,128)(2,1)} %copy-done.2, f32[512,1536]{1,0:T(8,128)} %get-tuple-element.65.refs_4_, ...), custom_call_target="tpu_custom_call" | custom-call | flops 754974720 | bytes 2129920 | tf_op jit(solution)/shard_map/gradients/pallas_call | solution.py:200
  (37 shorter events, 0.1 us)
Async XLA Ops:
  4.2 24.7 %collective-permute-start.1 = (bf16[40,4096]{1,0:T(8,128)(2,1)}, bf16[40,4096]{1,0:T(8,128)(2,1)S(1)}, u32[]{:S(2)}, u32[]{:S(2)}) collective-permute-start(bf16[40,4096]{1,0:T(8,128)(2,1)} %get-tuple-element.40), channel_id=1, source_target_pairs={{0,2},{1,3},{2,0},{3,1},{4,6},{5,7},{6,4},{7,5},{8,10},{9,11},{10,... | collective-permute-start | bytes 983048 | tf_op jit(solution)/shard_map/ppermute | solution.py:225
  7.2 27.1 %collective-permute-start.2 = (bf16[40,4096]{1,0:T(8,128)(2,1)}, bf16[40,4096]{1,0:T(8,128)(2,1)S(1)}, u32[]{:S(2)}, u32[]{:S(2)}) collective-permute-start(bf16[40,4096]{1,0:T(8,128)(2,1)} %get-tuple-element.41), channel_id=1, source_target_pairs={{0,3},{1,2},{2,1},{3,0},{4,7},{5,6},{6,5},{7,4},{8,11},{9,10},{10,... | collective-permute-start | bytes 983048 | tf_op jit(solution)/shard_map/ppermute | solution.py:225
  7.2 36.6 %collective-permute-start.3 = (bf16[40,4096]{1,0:T(8,128)(2,1)}, bf16[40,4096]{1,0:T(8,128)(2,1)S(1)}, u32[]{:S(2)}, u32[]{:S(2)}) collective-permute-start(bf16[40,4096]{1,0:T(8,128)(2,1)} %get-tuple-element.43), channel_id=1, source_target_pairs={{0,4},{1,5},{2,6},{3,7},{4,0},{5,1},{6,2},{7,3},{8,12},{9,13},{10,... | collective-permute-start | bytes 983048 | tf_op jit(solution)/shard_map/ppermute | solution.py:225
  9.8 43.4 %collective-permute-start.4 = (bf16[40,4096]{1,0:T(8,128)(2,1)}, bf16[40,4096]{1,0:T(8,128)(2,1)S(1)}, u32[]{:S(2)}, u32[]{:S(2)}) collective-permute-start(bf16[40,4096]{1,0:T(8,128)(2,1)} %get-tuple-element.44), channel_id=1, source_target_pairs={{0,5},{1,4},{2,7},{3,6},{4,1},{5,0},{6,3},{7,2},{8,13},{9,12},{10,... | collective-permute-start | bytes 983048 | tf_op jit(solution)/shard_map/ppermute | solution.py:225
  10.0 52.4 %collective-permute-start = (bf16[40,4096]{1,0:T(8,128)(2,1)}, bf16[40,4096]{1,0:T(8,128)(2,1)S(1)}, u32[]{:S(2)}, u32[]{:S(2)}) collective-permute-start(bf16[40,4096]{1,0:T(8,128)(2,1)} %get-tuple-element.38), channel_id=1, source_target_pairs={{0,1},{1,0},{2,3},{3,2},{4,5},{5,4},{6,7},{7,6},{8,9},{9,8},{10,11... | collective-permute-start | bytes 983048 | tf_op jit(solution)/shard_map/ppermute | solution.py:225
  29.0 7.4 %copy-start.18 = (bf16[40,4096]{1,0:T(8,128)(2,1)}, bf16[40,4096]{1,0:T(8,128)(2,1)S(1)}, u32[]{:S(2)}) copy-start(bf16[40,4096]{1,0:T(8,128)(2,1)S(1)} %collective-permute-done.1.a_ref) | copy-start | bytes 983044
  29.0 35.2 %collective-permute-start.5 = (bf16[40,4096]{1,0:T(8,128)(2,1)}, bf16[40,4096]{1,0:T(8,128)(2,1)S(1)}, u32[]{:S(2)}, u32[]{:S(2)}) collective-permute-start(bf16[40,4096]{1,0:T(8,128)(2,1)} %get-tuple-element.46), channel_id=1, source_target_pairs={{0,6},{1,7},{2,4},{3,5},{4,2},{5,3},{6,0},{7,1},{8,14},{9,15},{10,... | collective-permute-start | bytes 983048 | tf_op jit(solution)/shard_map/ppermute | solution.py:225
  34.3 2.0 %copy-start.19 = (bf16[40,4096]{1,0:T(8,128)(2,1)}, bf16[40,4096]{1,0:T(8,128)(2,1)S(1)}, u32[]{:S(2)}) copy-start(bf16[40,4096]{1,0:T(8,128)(2,1)S(1)} %collective-permute-done.2.b_ref) | copy-start | bytes 983044
  34.3 39.1 %collective-permute-start.6 = (bf16[40,4096]{1,0:T(8,128)(2,1)}, bf16[40,4096]{1,0:T(8,128)(2,1)S(1)}, u32[]{:S(2)}, u32[]{:S(2)}) collective-permute-start(bf16[40,4096]{1,0:T(8,128)(2,1)} %get-tuple-element.47), channel_id=1, source_target_pairs={{0,7},{1,6},{2,5},{3,4},{4,3},{5,2},{6,1},{7,0},{8,15},{9,14},{10,... | collective-permute-start | bytes 983048 | tf_op jit(solution)/shard_map/ppermute | solution.py:225
  43.9 11.0 %copy-start.16 = (bf16[40,4096]{1,0:T(8,128)(2,1)}, bf16[40,4096]{1,0:T(8,128)(2,1)S(1)}, u32[]{:S(2)}) copy-start(bf16[40,4096]{1,0:T(8,128)(2,1)S(1)} %collective-permute-done.3.a_ref) | copy-start | bytes 983044
  43.9 30.9 %collective-permute-start.13 = (bf16[80,3328]{1,0:T(8,128)(2,1)}, bf16[80,3328]{1,0:T(8,128)(2,1)S(1)}, u32[]{:S(2)}, u32[]{:S(2)}) collective-permute-start(bf16[80,3328]{1,0:T(8,128)(2,1)} %get-tuple-element.58), channel_id=1, source_target_pairs={{0,8},{8,0},{16,24},{24,16},{1,9},{9,1},{17,25},{25,17},{2,10},{10... | collective-permute-start | bytes 1597448 | tf_op jit(solution)/shard_map/ppermute | solution.py:225
  53.3 1.6 %copy-start.17 = (bf16[40,4096]{1,0:T(8,128)(2,1)}, bf16[40,4096]{1,0:T(8,128)(2,1)S(1)}, u32[]{:S(2)}) copy-start(bf16[40,4096]{1,0:T(8,128)(2,1)S(1)} %collective-permute-done.4.b_ref) | copy-start | bytes 983044
  53.3 26.5 %collective-permute-start.14 = (bf16[80,3328]{1,0:T(8,128)(2,1)}, bf16[80,3328]{1,0:T(8,128)(2,1)S(1)}, u32[]{:S(2)}, u32[]{:S(2)}) collective-permute-start(bf16[80,3328]{1,0:T(8,128)(2,1)} %get-tuple-element.59), channel_id=1, source_target_pairs={{0,16},{8,24},{16,0},{24,8},{1,17},{9,25},{17,1},{25,9},{2,18},{10... | collective-permute-start | bytes 1597448 | tf_op jit(solution)/shard_map/ppermute | solution.py:225
  62.4 2.2 %copy-start.14 = (bf16[40,4096]{1,0:T(8,128)(2,1)}, bf16[40,4096]{1,0:T(8,128)(2,1)S(1)}, u32[]{:S(2)}) copy-start(bf16[40,4096]{1,0:T(8,128)(2,1)S(1)} %collective-permute-done.b_ref) | copy-start | bytes 983044
  62.4 27.5 %collective-permute-start.15 = (bf16[80,3328]{1,0:T(8,128)(2,1)}, bf16[80,3328]{1,0:T(8,128)(2,1)S(1)}, u32[]{:S(2)}, u32[]{:S(2)}) collective-permute-start(bf16[80,3328]{1,0:T(8,128)(2,1)} %get-tuple-element.60), channel_id=1, source_target_pairs={{0,24},{8,16},{16,8},{24,0},{1,25},{9,17},{17,9},{25,1},{2,26},{10... | collective-permute-start | bytes 1597448 | tf_op jit(solution)/shard_map/ppermute | solution.py:225
  64.1 8.1 %copy-start.13 = (bf16[40,4096]{1,0:T(8,128)(2,1)}, bf16[40,4096]{1,0:T(8,128)(2,1)S(1)}, u32[]{:S(2)}) copy-start(bf16[40,4096]{1,0:T(8,128)(2,1)S(1)} %collective-permute-done.5.a_ref) | copy-start | bytes 983044
  64.1 27.4 %collective-permute-start.16 = (bf16[80,3328]{1,0:T(8,128)(2,1)}, bf16[80,3328]{1,0:T(8,128)(2,1)S(1)}, u32[]{:S(2)}, u32[]{:S(2)}) collective-permute-start(bf16[80,3328]{1,0:T(8,128)(2,1)} %get-tuple-element.62), channel_id=1, source_target_pairs={{0,8},{8,0},{16,24},{24,16},{1,9},{9,1},{17,25},{25,17},{2,10},{10... | collective-permute-start | bytes 1597448 | tf_op jit(solution)/shard_map/ppermute | solution.py:225
  64.7 7.6 %copy-start.3 = (f32[80,1]{1,0:T(8,128)S(1)}, f32[80,1]{1,0:T(8,128)}, u32[]{:S(2)}) copy-start(f32[80,1]{1,0:T(8,128)} %get-tuple-element.42) | copy-start | bytes 964
  64.7 7.7 %copy-start.4 = (f32[80,1]{1,0:T(8,128)S(1)}, f32[80,1]{1,0:T(8,128)}, u32[]{:S(2)}) copy-start(f32[80,1]{1,0:T(8,128)} %get-tuple-element.45) | copy-start | bytes 964
  73.4 6.4 %copy-start.15 = (bf16[40,4096]{1,0:T(8,128)(2,1)}, bf16[40,4096]{1,0:T(8,128)(2,1)S(1)}, u32[]{:S(2)}) copy-start(bf16[40,4096]{1,0:T(8,128)(2,1)S(1)} %collective-permute-done.6.b_ref) | copy-start | bytes 983044
  73.4 45.7 %collective-permute-start.17 = (bf16[80,3328]{1,0:T(8,128)(2,1)}, bf16[80,3328]{1,0:T(8,128)(2,1)S(1)}, u32[]{:S(2)}, u32[]{:S(2)}) collective-permute-start(bf16[80,3328]{1,0:T(8,128)(2,1)} %get-tuple-element.63), channel_id=1, source_target_pairs={{0,16},{8,24},{16,0},{24,8},{1,17},{9,25},{17,1},{25,9},{2,18},{10... | collective-permute-start | bytes 1597448 | tf_op jit(solution)/shard_map/ppermute | solution.py:225
  74.8 14.2 %copy-start.7 = (bf16[80,3328]{1,0:T(8,128)(2,1)}, bf16[80,3328]{1,0:T(8,128)(2,1)S(1)}, u32[]{:S(2)}) copy-start(bf16[80,3328]{1,0:T(8,128)(2,1)S(1)} %collective-permute-done.13.refs_5_) | copy-start | bytes 1597444
  74.8 45.8 %collective-permute-start.18 = (bf16[80,3328]{1,0:T(8,128)(2,1)}, bf16[80,3328]{1,0:T(8,128)(2,1)}, u32[]{:S(2)}, u32[]{:S(2)}) collective-permute-start(bf16[80,3328]{1,0:T(8,128)(2,1)} %get-tuple-element.64), channel_id=1, source_target_pairs={{0,24},{8,16},{16,8},{24,0},{1,25},{9,17},{17,9},{25,1},{2,26},{10... | collective-permute-start | bytes 1597448 | tf_op jit(solution)/shard_map/ppermute | solution.py:225
  79.8 9.2 %copy-start.8 = (bf16[80,3328]{1,0:T(8,128)(2,1)}, bf16[80,3328]{1,0:T(8,128)(2,1)S(1)}, u32[]{:S(2)}) copy-start(bf16[80,3328]{1,0:T(8,128)(2,1)S(1)} %collective-permute-done.14.refs_6_) | copy-start | bytes 1597444
  79.8 11.7 %copy-start.11 = (bf16[80,3328]{1,0:T(8,128)(2,1)S(1)}, bf16[80,3328]{1,0:T(8,128)(2,1)}, u32[]{:S(2)}) copy-start(bf16[80,3328]{1,0:T(8,128)(2,1)} %get-tuple-element.56) | copy-start | bytes 1597444
  79.8 42.9 %copy-start.6 = (s32[2,128]{1,0:T(2,128)S(1)}, s32[2,128]{1,0:T(2,128)}, u32[]{:S(2)}) copy-start(s32[2,128]{1,0:T(2,128)} %get-tuple-element.36) | copy-start | bytes 3076
  79.8 43.0 %copy-start.5 = (f32[128,2]{0,1:T(2,128)S(1)}, f32[128,2]{0,1:T(2,128)}, u32[]{:S(2)}) copy-start(f32[128,2]{0,1:T(2,128)} %param.8) | copy-start | bytes 3076
  79.8 42.5 %collective-permute-start.10 = (bf16[80,3328]{1,0:T(8,128)(2,1)}, bf16[80,3328]{1,0:T(8,128)(2,1)}, u32[]{:S(2)}, u32[]{:S(2)}) collective-permute-start(bf16[80,3328]{1,0:T(8,128)(2,1)} %get-tuple-element.54), channel_id=1, source_target_pairs={{0,8},{8,0},{16,24},{24,16},{1,9},{9,1},{17,25},{25,17},{2,10},{10... | collective-permute-start | bytes 1597448 | tf_op jit(solution)/shard_map/ppermute | solution.py:225
  89.9 35.6 %copy-start.9 = (bf16[80,3328]{1,0:T(8,128)(2,1)}, bf16[80,3328]{1,0:T(8,128)(2,1)S(1)}, u32[]{:S(2)}) copy-start(bf16[80,3328]{1,0:T(8,128)(2,1)S(1)} %collective-permute-done.15.refs_7_) | copy-start | bytes 1597444
  89.9 35.6 %collective-permute-start.11 = (bf16[80,3328]{1,0:T(8,128)(2,1)}, bf16[80,3328]{1,0:T(8,128)(2,1)}, u32[]{:S(2)}, u32[]{:S(2)}) collective-permute-start(bf16[80,3328]{1,0:T(8,128)(2,1)} %get-tuple-element.55), channel_id=1, source_target_pairs={{0,16},{8,24},{16,0},{24,8},{1,17},{9,25},{17,1},{25,9},{2,18},{10... | collective-permute-start | bytes 1597448 | tf_op jit(solution)/shard_map/ppermute | solution.py:225
  91.5 34.0 %copy-start.10 = (bf16[80,3328]{1,0:T(8,128)(2,1)}, bf16[80,3328]{1,0:T(8,128)(2,1)S(1)}, u32[]{:S(2)}) copy-start(bf16[80,3328]{1,0:T(8,128)(2,1)S(1)} %collective-permute-done.16.refs_9_) | copy-start | bytes 1597444
  91.5 34.0 %collective-permute-start.12 = (bf16[80,3328]{1,0:T(8,128)(2,1)S(1)}, bf16[80,3328]{1,0:T(8,128)(2,1)}, u32[]{:S(2)}, u32[]{:S(2)}) collective-permute-start(bf16[80,3328]{1,0:T(8,128)(2,1)S(1)} %copy-done.11), channel_id=1, source_target_pairs={{0,24},{8,16},{16,8},{24,0},{1,25},{9,17},{17,9},{25,1},{2,26},{10... | collective-permute-start | bytes 1597448 | tf_op jit(solution)/shard_map/ppermute | solution.py:225
  119.1 6.4 %copy-start.12 = (bf16[80,3328]{1,0:T(8,128)(2,1)}, bf16[80,3328]{1,0:T(8,128)(2,1)S(1)}, u32[]{:S(2)}) copy-start(bf16[80,3328]{1,0:T(8,128)(2,1)S(1)} %collective-permute-done.17.refs_10_) | copy-start | bytes 1597444
  119.1 15.8 %collective-permute-start.7 = (bf16[80,3328]{1,0:T(8,128)(2,1)}, bf16[80,3328]{1,0:T(8,128)(2,1)S(1)}, u32[]{:S(2)}, u32[]{:S(2)}) collective-permute-start(bf16[80,3328]{1,0:T(8,128)(2,1)} %get-tuple-element.50), channel_id=1, source_target_pairs={{0,8},{8,0},{16,24},{24,16},{1,9},{9,1},{17,25},{25,17},{2,10},{10... | collective-permute-start | bytes 1597448 | tf_op jit(solution)/shard_map/ppermute | solution.py:225
  120.6 27.3 %collective-permute-start.8 = (bf16[80,3328]{1,0:T(8,128)(2,1)}, bf16[80,3328]{1,0:T(8,128)(2,1)S(1)}, u32[]{:S(2)}, u32[]{:S(2)}) collective-permute-start(bf16[80,3328]{1,0:T(8,128)(2,1)} %get-tuple-element.51), channel_id=1, source_target_pairs={{0,16},{8,24},{16,0},{24,8},{1,17},{9,25},{17,1},{25,9},{2,18},{10... | collective-permute-start | bytes 1597448 | tf_op jit(solution)/shard_map/ppermute | solution.py:225
  122.3 25.6 %collective-permute-start.9 = (bf16[80,3328]{1,0:T(8,128)(2,1)}, bf16[80,3328]{1,0:T(8,128)(2,1)S(1)}, u32[]{:S(2)}, u32[]{:S(2)}) collective-permute-start(bf16[80,3328]{1,0:T(8,128)(2,1)} %get-tuple-element.52), channel_id=1, source_target_pairs={{0,24},{8,16},{16,8},{24,0},{1,25},{9,17},{17,9},{25,1},{2,26},{10... | collective-permute-start | bytes 1597448 | tf_op jit(solution)/shard_map/ppermute | solution.py:225
  134.9 13.0 %copy-start = (bf16[80,3328]{1,0:T(8,128)(2,1)}, bf16[80,3328]{1,0:T(8,128)(2,1)S(1)}, u32[]{:S(2)}) copy-start(bf16[80,3328]{1,0:T(8,128)(2,1)S(1)} %collective-permute-done.7.refs_1_) | copy-start | bytes 1597444
  147.9 0.8 copy-start.1
  147.9 1.0 copy-start.2

commit v2 on v1

--- a/solution.py
+++ b/solution.py
@@ -69,31 +69,30 @@
     )(ids, probs, tokens, cotangent)
 
 
-def expert_kernel(a_ref, b_ref, gate_ref, up_ref, down_ref, *rest):
-    groups = len(rest) - 4
-    message_refs, inner_ref, x_rows, s_rows, total = rest[:groups], *rest[groups:]
-    width = gate_ref.shape[0]
-    tile = gate_ref.shape[1]
-    half = tile * pl.num_programs(0)
-    quarter = width // groups
-    factors = message_refs[0].shape[1] - 2 * quarter
+def expert_kernel(parts, first, final, *refs):
+    row_refs, (gate_ref, up_ref, down_ref), refs = refs[:parts], refs[parts : parts + 3], refs[parts + 3 :]
+    if not first:
+        (acc_gate, acc_up, acc_down), refs = refs[:3], refs[3:]
+    if final:
+        (out_both, out_down, inner_ref), refs = refs[:3], refs[3:]
+    else:
+        (out_gate, out_up, out_down, inner_ref), refs = refs[:4], refs[4:]
+    x_rows, s_rows, x_turned, s_own, total = refs
+    width, tile = gate_ref.shape
+    quarter = out_down.shape[1]
     step = pl.program_id(0)
-    group = lax.axis_index("dp")
 
     @pl.when(step == 0)
     def _():
-        for rows, start in ((x_rows, 0), (s_rows, width)):
-            rows[...] = jnp.concatenate(
-                [
-                    a_ref[:, start : start + width].astype(F32),
-                    b_ref[:, start : start + width].astype(F32),
-                ],
-                axis=0,
-            ).astype(BF16)
-        for m in range(groups):
-            at = pl.multiple_of(jnp.bitwise_xor(group, m) * quarter, quarter)
-            message_refs[m][:, factors : factors + quarter] = x_rows[:, pl.ds(at, quarter)]
-            message_refs[m][:, factors + quarter :] = s_rows[:, pl.ds(at, quarter)]
+        own = pl.multiple_of(lax.axis_index("dp") * quarter, quarter)
+        at = 0
+        for ref in row_refs:
+            count = ref.shape[0]
+            x_rows[at : at + count, :] = ref[:, :width]
+            s_rows[at : at + count, :] = ref[:, width:]
+            at += count
+        x_turned[...] = x_rows[:, pl.ds(own, quarter)].T
+        s_own[...] = s_rows[:, pl.ds(own, quarter)]
         total[...] = jnp.zeros_like(total)
 
     x, s = x_rows[...], s_rows[...]
@@ -108,116 +107,83 @@
     grad_gate = (grad_hidden * up * sigmoid * (1.0 + gate * (1.0 - sigmoid))).astype(BF16)
     grad_up = (grad_hidden * activated).astype(BF16)
     total[...] += jnp.sum(hidden.astype(F32) * grad_hidden, axis=1, keepdims=True)
-    for part, values in enumerate((grad_gate, grad_up, hidden)):
-        at = pl.multiple_of(part * half + step * tile, tile)
-        for message in message_refs:
-            message[:, pl.ds(at, tile)] = values
+    sum_gate = jnp.dot(x_turned[...], grad_gate, preferred_element_type=F32)
+    sum_up = jnp.dot(x_turned[...], grad_up, preferred_element_type=F32)
+    sum_down = jnp.dot(hidden.T, s_own[...], preferred_element_type=F32)
+    if not first:
+        sum_gate, sum_up, sum_down = (
+            sum_gate + acc_gate[...],
+            sum_up + acc_up[...],
+            sum_down + acc_down[...],
+        )
+    if final:
+        at = pl.multiple_of(step * tile, tile)
+        half = out_both.shape[1] // 2
+        out_both[:, pl.ds(at, tile)] = sum_gate.astype(BF16)
+        out_both[:, pl.ds(pl.multiple_of(half + at, tile), tile)] = sum_up.astype(BF16)
+    else:
+        out_gate[...] = sum_gate
+        out_up[...] = sum_up
+    out_down[...] = sum_down.astype(out_down.dtype)
 
     @pl.when(step == pl.num_programs(0) - 1)
     def _():
         inner_ref[...] = total[...]
 
 
-def expert_rows(rows_a, rows_b, weight_gu, weight_down, groups):
+def expert_rows(rows, weight_gu, weight_down, groups, sums=None, final=False):
     width, both = weight_gu.shape
     half = both // 2
+    quarter = width // groups
     tile = 256
     steps = half // tile
-    count = 2 * CAP
-    message = jax.ShapeDtypeStruct((count, 3 * half + 2 * (width // groups)), BF16)
+    count = sum(part.shape[0] for part in rows)
 
     def whole(shape):
         return pl.BlockSpec(shape, lambda h: (0, 0))
 
-    return pl.pallas_call(
-        expert_kernel,
+    sum_specs = [
+        pl.BlockSpec((quarter, tile), lambda h: (0, h)),
+        pl.BlockSpec((quarter, tile), lambda h: (0, h)),
+        pl.BlockSpec((tile, quarter), lambda h: (h, 0)),
+    ]
+    *sums_out, inner = pl.pallas_call(
+        functools.partial(expert_kernel, len(rows), sums is None, final),
         grid=(steps,),
-        in_specs=[
-            whole(rows_a.shape),
-            whole(rows_b.shape),
+        in_specs=[whole(part.shape) for part in rows]
+        + [
             pl.BlockSpec((width, tile), lambda h: (0, h)),
             pl.BlockSpec((width, tile), lambda h: (0, h + steps)),
             pl.BlockSpec((tile, width), lambda h: (h, 0)),
+        ]
+        + ([] if sums is None else sum_specs),
+        out_specs=([whole((quarter, both))] if final else sum_specs[:2])
+        + [sum_specs[2], whole((count, 1))],
+        out_shape=(
+            [jax.ShapeDtypeStruct((quarter, both), BF16)]
+            if final
+            else [jax.ShapeDtypeStruct((quarter, half), F32)] * 2
+        )
+        + [
+            jax.ShapeDtypeStruct((half, quarter), BF16 if final else F32),
+            jax.ShapeDtypeStruct((count, 1), F32),
         ],
-        out_specs=[whole(message.shape)] * groups + [whole((count, 1))],
-        out_shape=[message] * groups + [jax.ShapeDtypeStruct((count, 1), F32)],
         scratch_shapes=[
             pltpu.VMEM((count, width), BF16),
             pltpu.VMEM((count, width), BF16),
+            pltpu.VMEM((quarter, count), BF16),
+            pltpu.VMEM((count, quarter), BF16),
             pltpu.VMEM((count, 1), F32),
         ],
         compiler_params=pltpu.CompilerParams(vmem_limit_bytes=VMEM_LIMIT),
         cost_estimate=pl.CostEstimate(
-            flops=2 * 256 * width * 3 * half * 2,
-            bytes_accessed=2 * width * 3 * half,
+            flops=2 * count * (width + quarter) * 3 * half,
+            bytes_accessed=2 * width * 3 * half + 2 * 4 * quarter * 3 * half,
             transcendentals=count * half,
         ),
         name="expert_rows",
-    )(rows_a, rows_b, weight_gu, weight_gu, weight_down)
-
-
-def gradient_kernel(pieces, half, final, *refs):
-    piece_refs = refs[:pieces]
-    if final:
-        acc_gu, acc_down, out_gu, out_down, rows, turned, sems = refs[pieces:]
-    else:
-        out_gu, out_down, rows, turned, sems = refs[pieces:]
-    count = piece_refs[0].shape[0]
-    quarter = out_gu.shape[0]
-    copies = [
-        pltpu.make_async_copy(ref, rows.at[pl.ds(n * count, count), :], sems.at[n])
-        for n, ref in enumerate(piece_refs)
-    ]
-    for copy in copies:
-        copy.start()
-    for copy in copies:
-        copy.wait()
-    factors = 3 * half
-    tile = 256
-    turned[...] = rows[:, factors : factors + quarter].T
-    for at in range(0, 2 * half, tile):
-        grad = jnp.dot(turned[...], rows[:, at : at + tile], preferred_element_type=F32)
-        if final:
-            grad = grad + acc_gu[:, at : at + tile]
-        out_gu[:, at : at + tile] = grad.astype(out_gu.dtype)
-    for at in range(0, half, tile):
-        grad = jnp.dot(
-            rows[:, 2 * half + at : 2 * half + at + tile].T,
-            rows[:, factors + quarter :],
-            preferred_element_type=F32,
-        )
-        if final:
-            grad = grad + acc_down[at : at + tile, :]
-        out_down[at : at + tile, :] = grad.astype(out_down.dtype)
-
-
-def gradients(pieces, half, quarter, sums=None):
-    final = sums is not None
-    kept = BF16 if final else F32
-    count, message = pieces[0].shape
-    rows = count * len(pieces)
-    vmem = pl.BlockSpec(memory_space=pltpu.VMEM)
-    return pl.pallas_call(
-        functools.partial(gradient_kernel, len(pieces), half, final),
-        in_specs=[pl.BlockSpec(memory_space=pl.ANY)] * len(pieces) + ([vmem] * 2 if final else []),
-        out_specs=[vmem] * 2,
-        out_shape=[
-            jax.ShapeDtypeStruct((quarter, 2 * half), kept),
-            jax.ShapeDtypeStruct((half, quarter), kept),
-        ],
-        scratch_shapes=[
-            pltpu.VMEM((rows, message), BF16),
-            pltpu.VMEM((quarter, rows), BF16),
-            pltpu.SemaphoreType.DMA((len(pieces),)),
-        ],
-        compiler_params=pltpu.CompilerParams(vmem_limit_bytes=VMEM_LIMIT),
-        cost_estimate=pl.CostEstimate(
-            flops=2 * rows * quarter * 3 * half,
-            bytes_accessed=2 * rows * message,
-            transcendentals=0,
-        ),
-        name="gradients",
-    )(*pieces, *(sums or ()))
+    )(*rows, weight_gu, weight_gu, weight_down, *(sums or ()))
+    return sums_out, inner
 
 
 def exchange(values, axis, mask):
@@ -225,30 +191,42 @@
     return lax.ppermute(values, axis, [(n, n ^ mask) for n in range(size)])
 
 
+def swap(values):
+    return lax.all_to_all(values, "expert", split_axis=0, concat_axis=0, tiled=True)
+
+
 def plane_body(tokens, cotangent, gate_probs, expert_ids, gate_up, down):
     groups = lax.axis_size("dp")
+    group = lax.axis_index("dp")
     me = lax.axis_index("expert")
-    half = gate_up.shape[2] // 2
-    quarter = tokens.shape[1] // groups
     ids, probs = expert_ids.T, gate_probs.T
     *local, slots = dispatch_rows(ids, probs, tokens, cotangent)
     arrived = [local[0]] + [exchange(local[k], "expert", k) for k in range(1, EXPERTS)]
-    pieces, inner = [], []
-    for chunk in range(EXPERTS // 2):
-        *messages, chunk_inner = expert_rows(
-            arrived[2 * chunk], arrived[2 * chunk + 1], gate_up[0], down[0], groups
+    sums, inner = None, [None] * EXPERTS
+    chunks = (((0,), (1,)), ((2, 3),), ((4, 5),), ((6,), (7,)))
+    for number, chunk in enumerate(chunks):
+        rows = []
+        for part in chunk:
+            values = [arrived[k] for k in part]
+            values = values[0] if len(part) == 1 else jnp.concatenate(values, axis=0)
+            rows.append(lax.all_gather(values, "dp", tiled=True))
+        sums, found = expert_rows(
+            rows, gate_up[0], down[0], groups, sums, number == len(chunks) - 1
         )
-        inner.append(chunk_inner.reshape(-1))
-        pieces.append(
-            [messages[0]] + [exchange(messages[m], "dp", m) for m in range(1, groups)]
-        )
-    early = [piece for chunk in pieces[:-1] for piece in chunk]
-    sums = gradients(early, half, quarter)
-    grad_gu, grad_down = gradients(pieces[-1], half, quarter, tuple(sums))
-    gathered = lax.all_gather(jnp.concatenate(inner), "expert").reshape(EXPERTS, EXPERTS, CAP)
+        at = 0
+        for part in chunk:
+            size = groups * len(part) * CAP
+            own = lax.dynamic_index_in_dim(
+                found[at : at + size].reshape(groups, len(part), CAP), group, 0, keepdims=False
+            )
+            at += size
+            for n, k in enumerate(part):
+                inner[k] = own[n]
+    grad_gu, grad_down = sums
     numbers = jnp.arange(EXPERTS, dtype=jnp.int32)
-    mine = numbers[:, None] == jnp.bitwise_xor(numbers, me)[None, :]
-    returned = jnp.sum(jnp.where(mine[:, :, None], gathered, 0.0), axis=0).reshape(-1)
+    mine = (numbers[:, None] == jnp.bitwise_xor(numbers, me)[None, :])[:, :, None]
+    sent = jnp.sum(jnp.where(mine, jnp.stack(inner)[None], 0.0), axis=1)
+    returned = jnp.sum(jnp.where(mine, swap(sent)[None], 0.0), axis=1).reshape(-1)
     chosen = slots[:, None, :] == jnp.arange(EXPERTS * CAP, dtype=jnp.int32)[None, :, None]
     grad_probs = jnp.sum(jnp.where(chosen, returned[None, :, None], 0.0), axis=1) / probs
     return (grad_probs.T, grad_gu[None], grad_down[None])
@@ -259,10 +237,6 @@
     spread = values.reshape((EXPERTS, 1, CAP) + tail)
     spread = jnp.broadcast_to(spread, (EXPERTS, slices, CAP) + tail)
     return spread.reshape((expert_count, CAP) + tail)
-
-
-def swap(values):
-    return lax.all_to_all(values, "expert", split_axis=0, concat_axis=0, tiled=True)
 
 
 def sliced_body(tokens, cotangent, gate_probs, expert_ids, gate_up, down):

time: 156 us -> 250 us (1.60)
  waiting for transfers between devices: 49.1 us -> 149 us
  blocking collectives: 26.9 us -> 9.96 us
  between operations: 1.38 us -> 14.3 us
  starting transfers between devices: 25.6 us -> 13.1 us
  Pallas kernels: 46.9 us -> 55.8 us
    all_gather x0 -> x6, waiting for transfers between devices: none -> 86.5 us  [plane_body(): rows.append(lax.all_gather(values, 'dp', tiled=True))]
    unnamed x1 -> x0, blocking collectives: 26.9 us -> none
    ppermute x19 -> x7, waiting for transfers between devices: 49.1 us -> 62.3 us  [exchange(): return lax.ppermute(values, axis, [(n, n ^ mask) for n in range(size)])]
    ppermute x19 -> x7, starting transfers between devices: 25.6 us -> 12.8 us  [exchange(): return lax.ppermute(values, axis, [(n, n ^ mask) for n in range(size)])]
    all_to_all x0 -> x1, blocking collectives: none -> 9.96 us  [swap(): lax.all_to_all(values, 'expert', split_axis=0, concat_axis=0, tiled=True)]
    pallas_call x6 -> x4, Pallas kernels: 43.3 us -> 52.2 us  [expert_rows(): pl.pallas_call(functools.partial(expert_kernel, len(rows), sums is None,...]
  transfers between devices with their start and end apart: 19 -> 13, of which waited for: 7 -> 11; matrix products, arithmetic and copies ran while one was open for 3% -> 1% of each run, Pallas kernels for 24% -> 16%
where the time goes in v2:
time: 250 us
  waiting for transfers between devices  149 us (60%)
  Pallas kernels  55.8 us (22%)
  between operations  14.3 us (6%)
  starting transfers between devices  13.1 us (5%)
  blocking collectives  9.96 us (4%)
  local copies, waits for them, and re-layouts  5 us (2%)
  other arithmetic  2.94 us (1%)
    all_gather x6, waiting for transfers between devices, plane_body(): rows.append(lax.all_gather(values, 'dp', tiled=True))  86.5 us
    ppermute x7, waiting for transfers between devices, exchange(): return lax.ppermute(values, axis, [(n, n ^ mask) for n in range(size)])  62.3 us
    pallas_call x4, Pallas kernels, expert_rows(): pl.pallas_call(functools.partial(expert_kernel, len(rows), sums is None,...  52.2 us
    ppermute x7, starting transfers between devices, exchange(): return lax.ppermute(values, axis, [(n, n ^ mask) for n in range(size)])  12.8 us
    all_to_all x1, blocking collectives, swap(): lax.all_to_all(values, 'expert', split_axis=0, concat_axis=0, tiled=True)  9.96 us
  transfers between devices with their start and end apart: 13, of which 11 were waited for; matrix products, arithmetic and copies ran while one was open for 1% of the time, Pallas kernels for 16%

profile of v2, /device:TPU:0, one launch (start us, length us, event | category | flops | bytes accessed | tf_op | source)
XLA Modules:
  0.0 250.0 jit_solution(17173690879445507746)
XLA Ops:
  7.2 0.0 all-gather.7.cloned.1.call-start
  7.2 3.6 %dispatch_rows.1 = (bf16[40,4096]{1,0:T(8,128)(2,1)}, bf16[40,4096]{1,0:T(8,128)(2,1)}, bf16[40,4096]{1,0:T(8,128)(2,1)}, bf16[40,4096]{1,0:T(8,128)(2,1)}, bf16...) custom-call(s32[2,128]{1,0:T(2,128)} %bitcast.45, ...), custom_call_target="tpu_custom_call" | custom-call | flops 335544320 | bytes 4000000 | tf_op jit(solution)/shard_map/dispatch_rows/pallas_call | solution.py:60
  10.8 0.0 all-gather.7.cloned.1.call-update
  10.8 0.0 all-gather.9.cloned.1.call-start
  10.9 0.5 collective-permute-start
  11.4 1.5 collective-permute-done
  12.9 0.7 copy-done
  13.6 0.0 all-gather.9.cloned.1.call-update
  13.6 0.0 all-gather.11.cloned.1.call-start
  13.7 3.0 %collective-permute-start.1 = (bf16[40,4096]{1,0:T(8,128)(2,1)}, bf16[40,4096]{1,0:T(8,128)(2,1)S(1)}, u32[]{:S(2)}, u32[]{:S(2)}) collective-permute-start(bf16[40,4096]{1,0:T(8,128)(2,1)} %get-tuple-element.31), channel_id=1, source_target_pairs={{0,2},{1,3},{2,0},{3,1},{4,6},{5,7},{6,4},{7,5},{8,10},{9,11},{10,... | collective-permute-start | bytes 983048 | tf_op jit(solution)/shard_map/ppermute | solution.py:191
  16.7 0.0 collective-permute-start.2
  16.7 8.7 %collective-permute-done.1 = bf16[40,4096]{1,0:T(8,128)(2,1)S(1)} collective-permute-done((bf16[40,4096]{1,0:T(8,128)(2,1)}, bf16[40,4096]{1,0:T(8,128)(2,1)S(1)}, u32[]{:S(2)}, u32[]{:S(2)}) %collective-permute-start.1) | collective-permute-done | bytes 327712 | tf_op jit(solution)/shard_map/ppermute | solution.py:191
  25.4 6.1 %collective-permute-done.2 = bf16[40,4096]{1,0:T(8,128)(2,1)S(1)} collective-permute-done((bf16[40,4096]{1,0:T(8,128)(2,1)}, bf16[40,4096]{1,0:T(8,128)(2,1)S(1)}, u32[]{:S(2)}, u32[]{:S(2)}) %collective-permute-start.2) | collective-permute-done | bytes 327712 | tf_op jit(solution)/shard_map/ppermute | solution.py:191
  31.4 0.9 pad_maximum_fusion
  32.3 0.0 all-gather.11.cloned.1.call-update
  32.3 0.0 all-gather.13.cloned.1.call-start
  32.4 0.0 copy-done.10
  32.4 2.5 %collective-permute-start.3 = (bf16[40,4096]{1,0:T(8,128)(2,1)S(1)}, bf16[40,4096]{1,0:T(8,128)(2,1)S(1)}, u32[]{:S(2)}, u32[]{:S(2)}) collective-permute-start(bf16[40,4096]{1,0:T(8,128)(2,1)S(1)} %copy-done.10), channel_id=1, source_target_pairs={{0,4},{1,5},{2,6},{3,7},{4,0},{5,1},{6,2},{7,3},{8,12},{9,13},{10,... | collective-permute-start | bytes 983048 | tf_op jit(solution)/shard_map/ppermute | solution.py:191
  34.9 0.0 copy-done.9
  34.9 0.3 collective-permute-start.4
  35.2 22.7 %collective-permute-done.3 = bf16[40,4096]{1,0:T(8,128)(2,1)S(1)} collective-permute-done((bf16[40,4096]{1,0:T(8,128)(2,1)S(1)}, bf16[40,4096]{1,0:T(8,128)(2,1)S(1)}, u32[]{:S(2)}, u32[]{:S(2)}) %collective-permute-start.3) | collective-permute-done | bytes 327712 | tf_op jit(solution)/shard_map/ppermute | solution.py:191
  57.9 6.1 %collective-permute-done.4 = bf16[40,4096]{1,0:T(8,128)(2,1)S(1)} collective-permute-done((bf16[40,4096]{1,0:T(8,128)(2,1)S(1)}, bf16[40,4096]{1,0:T(8,128)(2,1)S(1)}, u32[]{:S(2)}, u32[]{:S(2)}) %collective-permute-start.4) | collective-permute-done | bytes 327712 | tf_op jit(solution)/shard_map/ppermute | solution.py:191
  64.0 0.9 pad_maximum_fusion.1
  64.9 0.0 all-gather.13.cloned.1.call-update
  64.9 0.0 all-gather.15.cloned.1.call-start
  64.9 0.0 copy-done.8
  65.0 4.1 %collective-permute-start.5 = (bf16[40,4096]{1,0:T(8,128)(2,1)S(1)}, bf16[40,4096]{1,0:T(8,128)(2,1)S(1)}, u32[]{:S(2)}, u32[]{:S(2)}) collective-permute-start(bf16[40,4096]{1,0:T(8,128)(2,1)S(1)} %copy-done.8), channel_id=1, source_target_pairs={{0,6},{1,7},{2,4},{3,5},{4,2},{5,3},{6,0},{7,1},{8,14},{9,15},{10,... | collective-permute-start | bytes 983048 | tf_op jit(solution)/shard_map/ppermute | solution.py:191
  69.0 8.1 %collective-permute-done.5 = bf16[40,4096]{1,0:T(8,128)(2,1)S(1)} collective-permute-done((bf16[40,4096]{1,0:T(8,128)(2,1)S(1)}, bf16[40,4096]{1,0:T(8,128)(2,1)S(1)}, u32[]{:S(2)}, u32[]{:S(2)}) %collective-permute-start.5) | collective-permute-done | bytes 327712 | tf_op jit(solution)/shard_map/ppermute | solution.py:191
  77.1 0.7 copy-done.1
  77.9 0.0 all-gather.15.cloned.1.call-update
  77.9 0.0 all-gather.17.cloned.1.call-start
  77.9 0.0 copy-done.7
  77.9 2.4 collective-permute-start.6
  80.4 9.2 %collective-permute-done.6 = bf16[40,4096]{1,0:T(8,128)(2,1)S(1)} collective-permute-done((bf16[40,4096]{1,0:T(8,128)(2,1)S(1)}, bf16[40,4096]{1,0:T(8,128)(2,1)S(1)}, u32[]{:S(2)}, u32[]{:S(2)}) %collective-permute-start.6) | collective-permute-done | bytes 327712 | tf_op jit(solution)/shard_map/ppermute | solution.py:191
  89.6 0.7 copy-done.2
  90.3 0.0 all-gather.17.cloned.1.call-update
  90.4 0.0 all-gather.7.cloned.1.call-done.refs_0_
  90.4 0.0 all-gather.9.cloned.1.call-done.refs_1_
  90.4 12.2 %expert_rows.4 = (f32[512,768]{1,0:T(8,128)}, f32[512,768]{1,0:T(8,128)}, f32[768,512]{1,0:T(8,128)}, f32[320,1]{1,0:T(8,128)}) custom-call(bf16[160,4096]{1,0:T(8,128)(2,1)} %all-gather.7.cloned.1.call-done.refs_0_, bf16[160,4096]{1,0:T(8,128)(2,1)} %all-gather.9.cloned.1.call-done.refs_1_, bf16[2048,1536]{1,0:T(8,128)(2,1)} %bitcast.28, ...), custom_call_target="tpu_custom_call" | custom-call | flops 3774873600 | bytes 18874368 | tf_op jit(solution)/shard_map/expert_rows/pallas_call | solution.py:150
  102.6 1.1 slice_reduce_fusion.2
  103.7 0.1 reshape.58
  103.8 0.1 reshape.59
  103.9 10.8 %all-gather.11.cloned.1.call-done.refs_0_ = bf16[320,4096]{1,0:T(8,128)(2,1)} async-done(((bf16[80,4096]{1,0:T(8,128)(2,1)}), bf16[320,4096]{1,0:T(8,128)(2,1)}) %all-gather.11.cloned.1.call-update) | async-done | bytes 2621456 | tf_op jit(solution)/shard_map/all_gather | solution.py:212
  114.7 13.7 %expert_rows.5 = (f32[512,768]{1,0:T(8,128)}, f32[512,768]{1,0:T(8,128)}, f32[768,512]{1,0:T(8,128)}, f32[320,1]{1,0:T(8,128)}) custom-call(bf16[320,4096]{1,0:T(8,128)(2,1)} %all-gather.11.cloned.1.call-done.refs_0_, bf16[2048,1536]{1,0:T(8,128)(2,1)} %bitcast.30, bf16[2048,1536]{1,0:T(8,128)(2,1)} %bitcast.31, bf16[768,2048]{1,0:T(8,128)(2,1)} %bitcast.37, ...), custom_call_target="tpu_custom_call" | custom-call | flops 3774873600 | bytes 18874368 | tf_op jit(solution)/shard_map/expert_rows/pallas_call | solution.py:150
  128.4 28.2 %all-gather.13.cloned.1.call-done.refs_0_ = bf16[320,4096]{1,0:T(8,128)(2,1)} async-done(((bf16[80,4096]{1,0:T(8,128)(2,1)}), bf16[320,4096]{1,0:T(8,128)(2,1)}) %all-gather.13.cloned.1.call-update) | async-done | bytes 2621456 | tf_op jit(solution)/shard_map/all_gather | solution.py:212
  156.7 13.6 %expert_rows.6 = (f32[512,768]{1,0:T(8,128)}, f32[512,768]{1,0:T(8,128)}, f32[768,512]{1,0:T(8,128)}, f32[320,1]{1,0:T(8,128)}) custom-call(bf16[320,4096]{1,0:T(8,128)(2,1)} %all-gather.13.cloned.1.call-done.refs_0_, bf16[2048,1536]{1,0:T(8,128)(2,1)} %bitcast.32, bf16[2048,1536]{1,0:T(8,128)(2,1)} %bitcast.33, bf16[768,2048]{1,0:T(8,128)(2,1)} %bitcast.38, ...), custom_call_target="tpu_custom_call" | custom-call | flops 3774873600 | bytes 18874368 | tf_op jit(solution)/shard_map/expert_rows/pallas_call | solution.py:150
  170.3 16.9 %all-gather.15.cloned.1.call-done.refs_0_ = bf16[160,4096]{1,0:T(8,128)(2,1)} async-done(((bf16[40,4096]{1,0:T(8,128)(2,1)}), bf16[160,4096]{1,0:T(8,128)(2,1)}) %all-gather.15.cloned.1.call-update) | async-done | bytes 1310736 | tf_op jit(solution)/shard_map/all_gather | solution.py:212
  187.2 30.5 %all-gather.17.cloned.1.call-done.refs_1_ = bf16[160,4096]{1,0:T(8,128)(2,1)} async-done(((bf16[40,4096]{1,0:T(8,128)(2,1)}), bf16[160,4096]{1,0:T(8,128)(2,1)}) %all-gather.17.cloned.1.call-update) | async-done | bytes 1310736 | tf_op jit(solution)/shard_map/all_gather | solution.py:212
  217.7 12.7 %expert_rows.7 = (bf16[512,1536]{1,0:T(8,128)(2,1)}, bf16[768,512]{1,0:T(8,128)(2,1)}, f32[320,1]{1,0:T(8,128)}) custom-call(bf16[160,4096]{1,0:T(8,128)(2,1)} %all-gather.15.cloned.1.call-done.refs_0_, bf16[160,4096]{1,0:T(8,128)(2,1)} %all-gather.17.cloned.1.call-done.refs_1_, bf16[2048,1536]{1,0:T(8,128)(2,1)} %bitcast.34, bf16[2048,1536]{1,0:T(8,128)(2,1)} %bitcast.35, ...), custom_call_target="tpu_custom_call" | custom-call | flops 3774873600 | bytes 18874368 | tf_op jit(solution)/shard_map/expert_rows/pallas_call | solution.py:150
  230.4 1.1 slice_reduce_fusion
  231.5 0.1 reshape.62
  231.6 0.1 reshape.63
  231.7 0.0 copy-done.4
  231.7 0.2 reduce.3
  231.8 0.1 reshape.61
  231.9 0.0 copy-done.3
  231.9 0.1 reduce.2
  232.1 0.1 reshape.60
  232.3 0.1 select_reduce_fusion.2
  232.4 10.0 %all_to_all.9 = f32[8,1,40]{2,1,0:T(1,128)S(1)} all-to-all(f32[8,1,40]{2,1,0:T(1,128)S(1)} %bitcast.41), channel_id=1, replica_groups=mesh['dp'=4,'expert'=8] {'expert'}, dimensions={0} | all-to-all | bytes 2560 | tf_op jit(solution)/shard_map/all_to_all | solution.py:195
  242.3 0.1 select_reduce_fusion.1
  242.4 0.1 broadcast_in_dim.63
  242.5 0.1 select_reduce_fusion
  242.6 0.6 bitcast_divide_fusion
  (21 shorter events, 0.1 us)
Async XLA Ops:
  7.2 83.2 %all-gather.7.cloned.1.call-start = ((), (), s32[]{:S(2)}) async-start(), calls=%async_computation.1 | async-start | bytes 1638400 | tf_op jit(solution)/shard_map/all_gather | solution.py:212
  10.8 21.6 %copy-start.10 = (bf16[40,4096]{1,0:T(8,128)(2,1)S(1)}, bf16[40,4096]{1,0:T(8,128)(2,1)}, u32[]{:S(2)}) copy-start(bf16[40,4096]{1,0:T(8,128)(2,1)} %get-tuple-element.37) | copy-start | bytes 983044
  10.8 24.1 %copy-start.9 = (bf16[40,4096]{1,0:T(8,128)(2,1)S(1)}, bf16[40,4096]{1,0:T(8,128)(2,1)}, u32[]{:S(2)}) copy-start(bf16[40,4096]{1,0:T(8,128)(2,1)} %get-tuple-element.38) | copy-start | bytes 983044
  10.8 79.6 %all-gather.9.cloned.1.call-start = ((), (), s32[]{:S(2)}) async-start(), calls=%async_computation.2 | async-start | bytes 1638400 | tf_op jit(solution)/shard_map/all_gather | solution.py:212
  10.9 2.0 collective-permute-start
  12.9 0.7 copy-start
  13.6 101.1 %all-gather.11.cloned.1.call-start = ((), (), s32[]{:S(2)}) async-start(), calls=%async_computation.3 | async-start | bytes 3276800 | tf_op jit(solution)/shard_map/all_gather | solution.py:212
  13.7 11.7 %collective-permute-start.1 = (bf16[40,4096]{1,0:T(8,128)(2,1)}, bf16[40,4096]{1,0:T(8,128)(2,1)S(1)}, u32[]{:S(2)}, u32[]{:S(2)}) collective-permute-start(bf16[40,4096]{1,0:T(8,128)(2,1)} %get-tuple-element.31), channel_id=1, source_target_pairs={{0,2},{1,3},{2,0},{3,1},{4,6},{5,7},{6,4},{7,5},{8,10},{9,11},{10,... | collective-permute-start | bytes 983048 | tf_op jit(solution)/shard_map/ppermute | solution.py:191
  16.7 14.8 %collective-permute-start.2 = (bf16[40,4096]{1,0:T(8,128)(2,1)}, bf16[40,4096]{1,0:T(8,128)(2,1)S(1)}, u32[]{:S(2)}, u32[]{:S(2)}) collective-permute-start(bf16[40,4096]{1,0:T(8,128)(2,1)} %get-tuple-element.32), channel_id=1, source_target_pairs={{0,3},{1,2},{2,1},{3,0},{4,7},{5,6},{6,5},{7,4},{8,11},{9,10},{10,... | collective-permute-start | bytes 983048 | tf_op jit(solution)/shard_map/ppermute | solution.py:191
  32.3 32.6 %copy-start.8 = (bf16[40,4096]{1,0:T(8,128)(2,1)S(1)}, bf16[40,4096]{1,0:T(8,128)(2,1)}, u32[]{:S(2)}) copy-start(bf16[40,4096]{1,0:T(8,128)(2,1)} %get-tuple-element.43) | copy-start | bytes 983044
  32.3 45.6 %copy-start.7 = (bf16[40,4096]{1,0:T(8,128)(2,1)S(1)}, bf16[40,4096]{1,0:T(8,128)(2,1)}, u32[]{:S(2)}) copy-start(bf16[40,4096]{1,0:T(8,128)(2,1)} %get-tuple-element.44) | copy-start | bytes 983044
  32.3 124.3 %all-gather.13.cloned.1.call-start = ((), (), s32[]{:S(2)}) async-start(), calls=%async_computation.4 | async-start | bytes 3276800 | tf_op jit(solution)/shard_map/all_gather | solution.py:212
  32.4 25.5 %collective-permute-start.3 = (bf16[40,4096]{1,0:T(8,128)(2,1)S(1)}, bf16[40,4096]{1,0:T(8,128)(2,1)S(1)}, u32[]{:S(2)}, u32[]{:S(2)}) collective-permute-start(bf16[40,4096]{1,0:T(8,128)(2,1)S(1)} %copy-done.10), channel_id=1, source_target_pairs={{0,4},{1,5},{2,6},{3,7},{4,0},{5,1},{6,2},{7,3},{8,12},{9,13},{10,... | collective-permute-start | bytes 983048 | tf_op jit(solution)/shard_map/ppermute | solution.py:191
  34.9 29.1 %collective-permute-start.4 = (bf16[40,4096]{1,0:T(8,128)(2,1)S(1)}, bf16[40,4096]{1,0:T(8,128)(2,1)S(1)}, u32[]{:S(2)}, u32[]{:S(2)}) collective-permute-start(bf16[40,4096]{1,0:T(8,128)(2,1)S(1)} %copy-done.9), channel_id=1, source_target_pairs={{0,5},{1,4},{2,7},{3,6},{4,1},{5,0},{6,3},{7,2},{8,13},{9,12},{10,... | collective-permute-start | bytes 983048 | tf_op jit(solution)/shard_map/ppermute | solution.py:191
  64.9 122.3 %all-gather.15.cloned.1.call-start = ((), (), s32[]{:S(2)}) async-start(), calls=%async_computation.5 | async-start | bytes 1638400 | tf_op jit(solution)/shard_map/all_gather | solution.py:212
  65.0 12.1 %collective-permute-start.5 = (bf16[40,4096]{1,0:T(8,128)(2,1)S(1)}, bf16[40,4096]{1,0:T(8,128)(2,1)S(1)}, u32[]{:S(2)}, u32[]{:S(2)}) collective-permute-start(bf16[40,4096]{1,0:T(8,128)(2,1)S(1)} %copy-done.8), channel_id=1, source_target_pairs={{0,6},{1,7},{2,4},{3,5},{4,2},{5,3},{6,0},{7,1},{8,14},{9,15},{10,... | collective-permute-start | bytes 983048 | tf_op jit(solution)/shard_map/ppermute | solution.py:191
  77.1 0.7 copy-start.1
  77.9 139.8 %all-gather.17.cloned.1.call-start = ((), (), s32[]{:S(2)}) async-start(), calls=%async_computation.6 | async-start | bytes 1638400 | tf_op jit(solution)/shard_map/all_gather | solution.py:212
  77.9 11.7 %collective-permute-start.6 = (bf16[40,4096]{1,0:T(8,128)(2,1)S(1)}, bf16[40,4096]{1,0:T(8,128)(2,1)S(1)}, u32[]{:S(2)}, u32[]{:S(2)}) collective-permute-start(bf16[40,4096]{1,0:T(8,128)(2,1)S(1)} %copy-done.7), channel_id=1, source_target_pairs={{0,7},{1,6},{2,5},{3,4},{4,3},{5,2},{6,1},{7,0},{8,15},{9,14},{10,... | collective-permute-start | bytes 983048 | tf_op jit(solution)/shard_map/ppermute | solution.py:191
  89.6 0.7 copy-start.2
  217.7 14.0 %copy-start.4 = (f32[320,1]{1,0:T(8,128)S(1)}, f32[320,1]{1,0:T(8,128)}, u32[]{:S(2)}) copy-start(f32[320,1]{1,0:T(8,128)} %get-tuple-element.42) | copy-start | bytes 3844
  217.7 14.2 %copy-start.3 = (f32[320,1]{1,0:T(8,128)S(1)}, f32[320,1]{1,0:T(8,128)}, u32[]{:S(2)}) copy-start(f32[320,1]{1,0:T(8,128)} %get-tuple-element.36) | copy-start | bytes 3844
  217.7 24.8 %copy-start.6 = (s32[2,128]{1,0:T(2,128)S(1)}, s32[2,128]{1,0:T(2,128)}, u32[]{:S(2)}) copy-start(s32[2,128]{1,0:T(2,128)} %get-tuple-element.27) | copy-start | bytes 3076
  217.7 24.9 %copy-start.5 = (f32[128,2]{0,1:T(2,128)S(1)}, f32[128,2]{0,1:T(2,128)}, u32[]{:S(2)}) copy-start(f32[128,2]{0,1:T(2,128)} %param.8) | copy-start | bytes 3076
Sparse Core Ops, SparseCore 0:
  11.0 31.4 all-gather.6
  44.3 28.7 all-gather.8
  75.0 39.6 all-gather.10
  117.0 39.6 all-gather.12
  158.3 28.7 all-gather.14
  188.9 28.7 all-gather.16
